TPU v7x, 32 devices: a whole 2x2x4 slice. The times are simulated.
32 devices in a mesh: chan: 4 (over x, core), blk: 8 (over z, y).
Axes of the slice: x: 2, y: 2, z: 4, core: 2. Of those that a mesh axis runs over, the one named last changes fastest.
Arguments:
- t_matrix: bfloat16 [4, 1024, 1024], P('chan', 'blk'), may hold values from -0.1875 to 0.1875
- v_jacobi: bfloat16 [4, 1024, 1024], P('chan'), may hold values from -6 to 6
- channel_dims: int32 [4], P('chan'), may hold values from 128 to 1024, as said below
- owner_map: int32 [4], replicated, may hold values from 0 to 3, each once
Outputs:
- triplet_blocks: bfloat16 [4, 4, 1024, 256], P('chan', None, 'blk')
Inputs may be any that keep to these rules, and one draw needn't show every extreme that they name: `channel_dims`: channel 0 has exactly 1024 live states; others vary.
All inputs are finite; a program needn't handle non-finite values.
Results may differ from a plain program's by a relative error of at most 0.0058.
Values may be sent and summed in bfloat16 or wider, within the bound.
No kernel may reach another device: no remote copies, remote signals or barrier semaphores. Data moves between devices by JAX's collectives and lax.ppermute only.
A program may use at most 64 MiB of HBM per device.

v0:
```python
import jax
import jax.numpy as jnp
from jax import lax
from jax.sharding import PartitionSpec as P


def per_device(t_matrix, v_jacobi, channel_dims, owner_map):
    jac_width = v_jacobi.shape[2]
    positions = jnp.arange(jac_width, dtype=jnp.int32)
    kept_mask = (positions[None, :] < channel_dims[:, None]).astype(jnp.float32)
    v_float = v_jacobi.astype(jnp.float32)
    v_masked = (
        (v_float + jnp.swapaxes(v_float, 1, 2))
        * 0.5
        * kept_mask[:, :, None]
        * kept_mask[:, None, :]
    ).astype(jnp.bfloat16)
    weighted = jnp.einsum(
        "crj,cji->cri", t_matrix, v_masked, preferred_element_type=jnp.float32
    ).astype(jnp.bfloat16)
    groups = lax.axis_size("chan")
    owners = jnp.arange(groups, dtype=jnp.int32)
    source_block = jnp.sum(
        owners[None, :] * (owner_map[None, :] == owners[:, None]).astype(jnp.int32), axis=1
    )
    lab_rows = jnp.einsum(
        "cri,cpi->crp",
        weighted,
        lax.all_gather(t_matrix, "blk", axis=1, tiled=True),
        preferred_element_type=jnp.float32,
    ).astype(jnp.bfloat16)
    block_cols = lab_rows.shape[2] // groups
    col_blocks = lab_rows.reshape(lab_rows.shape[0], lab_rows.shape[1], groups, block_cols)
    picked = jnp.take(col_blocks, source_block, axis=2)
    outgoing = jnp.transpose(picked, (2, 0, 1, 3))
    return lax.all_to_all(outgoing, "chan", split_axis=0, concat_axis=1, tiled=True)


def solution(mesh):
    in_specs = (P("chan", "blk", None), P("chan", None, None), P("chan"), P())
    out_specs = P("chan", None, "blk", None)
    return jax.shard_map(
        per_device, mesh=mesh, in_specs=in_specs, out_specs=out_specs, check_vma=False
    )
```

profile of v0, /device:TPU:0, one launch (start us, length us, event | category | flops | bytes accessed | tf_op | source)
XLA Modules:
  0.0 83.7 jit_solution(13659853064048360835)
XLA Ops:
  6.5 0.0 copy-start.1
  6.5 0.0 copy-start
  6.5 0.0 copy-start.2
  6.5 0.0 all-gather.2.cloned.1.call-start
  6.5 0.7 all-gather.2.cloned.1.call-update
  7.9 4.1 %copy.11 = f32[1,1024,1024]{1,2,0:T(8,128)} copy(bf16[1,1024,1024]{2,1,0:T(8,128)(2,1)} %param.5) | data formatting | bytes 6291456 | tf_op jit(solution)/shard_map/convert_element_type | solution.py:11
  12.1 0.0 copy-done.2
  12.1 0.1 select_reduce_fusion
  12.2 49.3 %all-gather.2.cloned.1.call-done = bf16[1,1024,1024]{2,1,0:T(8,128)(2,1)} async-done(((bf16[1,128,1024]{2,1,0:T(8,128)(2,1)}), bf16[1,1024,1024]{2,1,0:T(8,128)(2,1)}) %all-gather.2.cloned.1.call-update) | async-done | bytes 2097168 | tf_op jit(solution)/shard_map/all_gather | solution.py:29
  61.5 0.0 copy-done.1
  61.5 0.0 copy-done
  61.5 5.4 %fusion.10 = bf16[128,1024]{1,0:T(8,128)(2,1)S(1)} fusion(bf16[1,1024,1024]{2,1,0:T(8,128)(2,1)} %all-gather.2.cloned.1.call-done, f32[1,1024,1024]{1,2,0:T(8,128)} %copy.11, f32[1024]{0:T(1024)S(1)} %fusion.22, f32[1024]{0:T(1024)S(1)} %fusion.23, bf16[1,1024,1024]{2,1,0:T(8,128)(2,1)S(1)} %copy-done, bf16[1,128,1024]{2,1,0:T(8,128)(2,1)S(1)} %copy-done.1), kind=kOutput, calls=%fused_computation.11 | convolution fusion | flops 542375936 | bytes 8921088 | tf_op jit(solution)/shard_map/cri,cpi->crp/dot_general | solution.py:26
  66.9 0.6 gather_fusion
  67.5 0.1 fusion.19
  67.6 8.6 %all_to_all.12 = bf16[4,1,128,256]{3,2,1,0:T(8,128)(2,1)S(1)} all-to-all(bf16[4,1,128,256]{3,2,1,0:T(8,128)(2,1)S(1)} %fusion.19), channel_id=1, replica_groups=mesh['chan'=4,'blk'=8] {'chan'}, dimensions={0} | all-to-all | bytes 524288 | tf_op jit(solution)/shard_map/all_to_all | solution.py:36
  76.2 0.7 copy.19
  (6 shorter events, 0.0 us)
Async XLA Ops:
  6.5 55.0 %copy-start.1 = (bf16[1,128,1024]{2,1,0:T(8,128)(2,1)S(1)}, bf16[1,128,1024]{2,1,0:T(8,128)(2,1)}, u32[]{:S(2)}) copy-start(bf16[1,128,1024]{2,1,0:T(8,128)(2,1)} %param.4) | copy-start | bytes 786436
  6.5 55.0 %copy-start = (bf16[1,1024,1024]{2,1,0:T(8,128)(2,1)S(1)}, bf16[1,1024,1024]{2,1,0:T(8,128)(2,1)}, u32[]{:S(2)}) copy-start(bf16[1,1024,1024]{2,1,0:T(8,128)(2,1)} %param.5) | copy-start | bytes 6291460
  6.5 5.5 %copy-start.2 = (s32[4]{0:T(128)S(1)}, s32[4]{0:T(128)}, u32[]{:S(2)}) copy-start(s32[4]{0:T(128)} %param.7) | copy-start | bytes 52
  6.5 55.0 %all-gather.2.cloned.1.call-start = ((), (), s32[]{:S(2)}) async-start(), calls=%async_computation.1 | async-start | bytes 2359296 | tf_op jit(solution)/shard_map/all_gather | solution.py:29
Sparse Core Ops, SparseCore 0:
  9.5 51.9 all-gather.1
where the time goes:
time: 83.9 us; the launch traced here: 83.7 us
  waiting for transfers between devices  50 us (60%)
  between operations  14.1 us (17%)
  blocking collectives  8.58 us (10%)
  local copies, waits for them, and re-layouts  5.43 us (6%)
  matrix products  5.37 us (6%)
    all_gather x1, waiting for transfers between devices, per_device(): lax.all_gather(t_matrix, 'blk', axis=1, tiled=True)  49.3 us
    all_to_all x1, blocking collectives, per_device(): lax.all_to_all(outgoing, 'chan', split_axis=0, concat_axis=1, tiled=True)  8.58 us
    dot_general x1, matrix products, per_device(): jnp.einsum('cri,cpi->crp', weighted, lax.all_gather(t_matrix, 'blk', axis...  5.37 us
    convert_element_type x1, local copies, waits for them, and re-layouts, per_device(): v_float = v_jacobi.astype(jnp.float32)  4.13 us
  transfers between devices with their start and end apart: 1, of which 1 were waited for; matrix products, arithmetic and copies ran while one was open for 5% of the time, Pallas kernels for 0%

commit v1 on v0

v1 whole, which is shorter than its diff:
```python
import functools

import jax
import jax.numpy as jnp
import numpy as np
from jax import lax
from jax.experimental import pallas as pl
from jax.experimental.pallas import tpu as pltpu
from jax.sharding import Mesh, PartitionSpec as P

F32 = jnp.float32
BF16 = jnp.bfloat16
VMEM_LIMIT = 48 * 1024 * 1024


def dot_nt(a, b):
    return lax.dot_general(a, b, (((1,), (1,)), ((), ())), preferred_element_type=F32)


def weights_kernel(live_ref, v_ref, *refs):
    n_rows = (len(refs) - 1) // 2
    t_refs, vm_ref, w_refs = refs[:n_rows], refs[n_rows], refs[n_rows + 1 :]
    width = v_ref.shape[0]
    tile = min(256, width)
    live = live_ref[0]
    for i in range(0, width, tile):
        row_live = lax.broadcasted_iota(jnp.int32, (tile, tile), 0) + i < live
        for j in range(0, width, tile):
            col_live = lax.broadcasted_iota(jnp.int32, (tile, tile), 1) + j < live
            here = v_ref[i : i + tile, j : j + tile].astype(F32)
            there = v_ref[j : j + tile, i : i + tile].astype(F32)
            mean = (here + there.T) * 0.5
            vm_ref[i : i + tile, j : j + tile] = jnp.where(row_live & col_live, mean, 0.0).astype(BF16)
    for t_ref, w_ref in zip(t_refs, w_refs):
        w_ref[...] = jnp.dot(t_ref[...], vm_ref[...], preferred_element_type=F32).astype(BF16)


def tiles_kernel(n_w, n_t, n_half, half, place_ref, *refs):
    w_refs, t_refs = refs[:n_w], refs[n_w : n_w + n_t]
    vm_ref = refs[n_w + n_t]
    h_refs = refs[n_w + n_t + 1 : n_w + n_t + 1 + n_half]
    out_ref, shares, picked = refs[n_w + n_t + 1 + n_half :]
    groups = n_half
    rows = w_refs[0].shape[0]
    for k, h_ref in enumerate(h_refs):
        shares[k] = h_ref[...]
    for d in range(groups):
        picked[d * half : (d + 1) * half, :] = shares[place_ref[d]]
    first = lax.broadcasted_iota(jnp.int32, (rows // 2, 2 * half), 1) < half
    for k in range(n_w + n_t):
        if k < n_w:
            left = w_refs[k][...]
        else:
            left = jnp.dot(t_refs[k - n_w][...], vm_ref[...], preferred_element_type=F32).astype(BF16)
        place = place_ref[groups + k]
        for pair in range(groups // 2):
            both = dot_nt(left, picked[pair * 2 * half : (pair + 1) * 2 * half, :])
            top, bottom = both[: rows // 2], both[rows // 2 :]
            even = jnp.where(first, top, pltpu.roll(bottom, half, 1))
            odd = jnp.where(first, pltpu.roll(top, half, 1), bottom)
            out_ref[2 * pair, place] = even.astype(BF16)
            out_ref[2 * pair + 1, place] = odd.astype(BF16)


def place_kernel(ny, half, swap_ref, in_ref, out_ref):
    channels = in_ref.shape[0]
    deep = in_ref.shape[2]
    first = lax.broadcasted_iota(jnp.int32, (deep, 2 * half), 1) < half
    swap = swap_ref[0] > 0
    for c in range(channels):
        for y in range(ny):
            zero, one = in_ref[c, y].astype(F32), in_ref[c, ny + y].astype(F32)
            a = jnp.where(swap, one, zero)
            b = jnp.where(swap, zero, one)
            top = jnp.where(first, a, pltpu.roll(b, half, 1))
            bottom = jnp.where(first, pltpu.roll(a, half, 1), b)
            out_ref[c, :deep, y * 2 * half : (y + 1) * 2 * half] = top.astype(BF16)
            out_ref[c, deep:, y * 2 * half : (y + 1) * 2 * half] = bottom.astype(BF16)


def xor_pairs(size, k):
    return [(i, i ^ k) for i in range(size)]


def per_device(t_matrix, v_jacobi, channel_dims, owner_map):
    t, v = t_matrix[0], v_jacobi[0]
    rows, width = t.shape
    half = rows // 2
    groups, nzg, ny = lax.axis_size("chan"), lax.axis_size("zg"), lax.axis_size("y")
    zg, zp, y = lax.axis_index("zg"), lax.axis_index("zp"), lax.axis_index("y")

    near = lax.ppermute(t, "zp", xor_pairs(2, 1))
    side = [lax.ppermute(t, "y", xor_pairs(ny, k)) for k in range(1, ny)]
    shares = [t[:half], None]
    for k in range(1, nzg):
        shares.append(lax.ppermute(t[:half], "zg", xor_pairs(nzg, k)))
        shares.append(lax.ppermute(t[half:], ("zg", "zp"), xor_pairs(2 * nzg, 2 * k + 1)))
    shares[1] = near[half:]
    cross = [lax.ppermute(near, "y", xor_pairs(ny, k)) for k in range(1, ny)]

    owners = jnp.arange(groups, dtype=jnp.int32)
    source = jnp.sum(owners[None, :] * (owner_map[None, :] == owners[:, None]).astype(jnp.int32), axis=1)
    share_at = source ^ (zg * 2 + zp)
    ry = np.arange(ny)
    row_at = [zp * ny + (y ^ ry), (1 - zp) * ny + (y ^ ry)]
    order = jnp.concatenate([row_at[0], row_at[1]]).astype(jnp.int32)
    place = jnp.concatenate([share_at.astype(jnp.int32), order])
    swap = jnp.sum(jnp.where(owners == lax.axis_index("chan"), source, 0)) & 1

    lefts = [t] + side + [near]
    smem, vmem = pl.BlockSpec(memory_space=pltpu.SMEM), pl.BlockSpec(memory_space=pltpu.VMEM)
    made = pl.pallas_call(
        weights_kernel,
        out_shape=[jax.ShapeDtypeStruct((width, width), BF16)]
        + [jax.ShapeDtypeStruct((rows, width), BF16)] * len(lefts),
        in_specs=[smem] + [vmem] * (1 + len(lefts)),
        out_specs=[vmem] * (1 + len(lefts)),
        compiler_params=pltpu.CompilerParams(vmem_limit_bytes=VMEM_LIMIT),
        cost_estimate=pl.CostEstimate(
            flops=2 * rows * width * width * len(lefts) + 4 * width * width,
            bytes_accessed=4 * width * width + 4 * rows * width * len(lefts),
            transcendentals=0,
        ),
    )(channel_dims, v, *lefts)
    vm, w = made[0], made[1:]
    n_t = len(cross)
    tiles = pl.pallas_call(
        functools.partial(tiles_kernel, len(w), n_t, len(shares), half),
        out_shape=jax.ShapeDtypeStruct((groups, 2 * ny, rows // 2, 2 * half), BF16),
        in_specs=[smem] + [vmem] * (len(w) + n_t + 1 + len(shares)),
        out_specs=vmem,
        scratch_shapes=[
            pltpu.VMEM((len(shares), half, width), BF16),
            pltpu.VMEM((groups * half, width), BF16),
        ],
        compiler_params=pltpu.CompilerParams(vmem_limit_bytes=VMEM_LIMIT),
        cost_estimate=pl.CostEstimate(
            flops=2 * rows * width * (width * n_t + groups * half * 2 * ny),
            bytes_accessed=2 * width * width + 4 * rows * width * 2 * ny,
            transcendentals=0,
        ),
    )(place, *w, *cross, vm, *shares)
    sent = tiles.reshape(groups * 2 * ny, rows // 2, 2 * half)
    got = lax.all_to_all(sent, ("chan", "zp", "y"), split_axis=0, concat_axis=0, tiled=True)
    got = got.reshape(groups, 2 * ny, rows // 2, 2 * half)
    out = pl.pallas_call(
        functools.partial(place_kernel, ny, half),
        out_shape=jax.ShapeDtypeStruct((groups, rows, ny * rows), BF16),
        in_specs=[smem, vmem],
        out_specs=vmem,
        compiler_params=pltpu.CompilerParams(vmem_limit_bytes=VMEM_LIMIT),
    )(swap.reshape(1), got)
    return out[None]


def solution(mesh):
    chan, blk = mesh.shape["chan"], mesh.shape["blk"]

    def whole(t_matrix, v_jacobi, channel_dims, owner_map):
        block_cols = t_matrix.shape[1] // chan
        ny = block_cols * blk // t_matrix.shape[1]
        inner = Mesh(mesh.devices.reshape(chan, blk // (2 * ny), 2, ny), ("chan", "zg", "zp", "y"))
        line = ("zg", "zp", "y")
        return jax.shard_map(
            per_device,
            mesh=inner,
            in_specs=(P("chan", line, None), P("chan", None, None), P("chan"), P()),
            out_specs=P("chan", None, line, None),
            check_vma=False,
        )(t_matrix, v_jacobi, channel_dims, owner_map)

    return whole
```

time: 83.9 us -> 34.6 us (0.41)
  waiting for transfers between devices: 50 us -> 11.3 us
  between operations: 14.1 us -> 1.28 us
  starting transfers between devices: 0.01 us -> 11.2 us
  blocking collectives: 8.58 us -> 0 us
  matrix products: 5.37 us -> 0 us
  Pallas kernels: 0 us -> 5.21 us
  local copies, waits for them, and re-layouts: 5.43 us -> 3.54 us
  other arithmetic: 0.24 us -> 1.48 us
    all_gather x1 -> x0, waiting for transfers between devices: 49.3 us -> none  [per_device(): lax.all_gather(t_matrix, 'blk', axis=1, tiled=True)]
    all_to_all x1 -> x0, blocking collectives: 8.58 us -> none  [per_device(): lax.all_to_all(outgoing, 'chan', split_axis=0, concat_axis=1, tiled=True)]
    ppermute x0 -> x5, starting transfers between devices: none -> 7.66 us  [the longest x1 2.97 us: per_device(): side = [lax.ppermute(t, 'y', xor_pairs(ny, k)) for k in range(1, ny)]]
    all_to_all x0 -> x1, waiting for transfers between devices: none -> 6.54 us  [per_device(): lax.all_to_all(sent, ('chan', 'zp', 'y'), split_axis=0, concat_axis=0, ti...]
    dot_general x1 -> x0, matrix products: 5.37 us -> none  [per_device(): jnp.einsum('cri,cpi->crp', weighted, lax.all_gather(t_matrix, 'blk', axis...]
    pallas_call x0 -> x3, Pallas kernels: none -> 5.21 us  [the longest x1 2.38 us: per_device(): pl.pallas_call(functools.partial(tiles_kernel, len(w), n_t, len(shares),...]
    ppermute x0 -> x5, waiting for transfers between devices: none -> 4.74 us  [the longest x1 3.92 us: per_device(): near = lax.ppermute(t, 'zp', xor_pairs(2, 1))]
    convert_element_type x1 -> x0, local copies, waits for them, and re-layouts: 4.13 us -> none  [per_device(): v_float = v_jacobi.astype(jnp.float32)]
  transfers between devices with their start and end apart: 1 -> 6, of which waited for: 1 -> 3; matrix products, arithmetic and copies ran while one was open for 5% -> 7% of each run, Pallas kernels for 0% -> 6%
where the time goes in v1:
time: 34.6 us; the launch traced here: 34 us
  waiting for transfers between devices  11.3 us (33%)
  starting transfers between devices  11.2 us (32%)
  Pallas kernels  5.21 us (15%)
  local copies, waits for them, and re-layouts  3.54 us (10%)
  other arithmetic  1.48 us (4%)
  between operations  1.28 us (4%)
    all_to_all x1, waiting for transfers between devices, per_device(): lax.all_to_all(sent, ('chan', 'zp', 'y'), split_axis=0, concat_axis=0, ti...  6.54 us
    ppermute x1, waiting for transfers between devices, per_device(): near = lax.ppermute(t, 'zp', xor_pairs(2, 1))  3.92 us
    all_to_all x1, starting transfers between devices, per_device(): lax.all_to_all(sent, ('chan', 'zp', 'y'), split_axis=0, concat_axis=0, ti...  3.53 us
    ppermute x1, starting transfers between devices, per_device(): side = [lax.ppermute(t, 'y', xor_pairs(ny, k)) for k in range(1, ny)]  2.97 us
    ppermute x1, starting transfers between devices, per_device(): shares.append(lax.ppermute(t[:half], 'zg', xor_pairs(nzg, k)))  2.65 us
    unnamed x4, local copies, waits for them, and re-layouts  2.54 us
    pallas_call x1, Pallas kernels, per_device(): pl.pallas_call(functools.partial(tiles_kernel, len(w), n_t, len(shares),...  2.38 us
    pallas_call x1, Pallas kernels, per_device(): pl.pallas_call(weights_kernel, out_shape=[jax.ShapeDtypeStruct((width, wi...  1.99 us
  transfers between devices with their start and end apart: 6, of which 3 were waited for; matrix products, arithmetic and copies ran while one was open for 7% of the time, Pallas kernels for 6%

profile of v1, /device:TPU:0, one launch (start us, length us, event | category | flops | bytes accessed | tf_op | source)
XLA Modules:
  0.0 34.0 jit_solution(4384275731918130819)
XLA Ops:
  0.0 3.0 %collective-permute-start = (bf16[128,1024]{1,0:T(8,128)(2,1)}, bf16[128,1024]{1,0:T(8,128)(2,1)S(1)}, u32[]{:S(2)}, u32[]{:S(2)}) collective-permute-start(bf16[128,1024]{1,0:T(8,128)(2,1)} %bitcast.11), channel_id=1, source_target_pairs={{0,1},{1,0},{2,3},{3,2},{4,5},{5,4},{6,7},{7,6},{8,9},{9,8},{10,11... | collective-permute-start | bytes 786440 | tf_op jit(solution)/shard_map/ppermute | solution.py:93
  3.0 1.6 %collective-permute-start.1 = (bf16[128,1024]{1,0:T(8,128)(2,1)}, bf16[128,1024]{1,0:T(8,128)(2,1)S(1)}, u32[]{:S(2)}, u32[]{:S(2)}) collective-permute-start(bf16[128,1024]{1,0:T(8,128)(2,1)} %bitcast.12), channel_id=1, source_target_pairs={{0,2},{2,0},{1,3},{3,1},{4,6},{6,4},{5,7},{7,5},{8,10},{10,8},{9,1... | collective-permute-start | bytes 786440 | tf_op jit(solution)/shard_map/ppermute | solution.py:92
  4.5 1.0 %slice_bitcast_fusion = (bf16[64,1024]{1,0:T(8,128)(2,1)S(1)}, bf16[64,1024]{1,0:T(8,128)(2,1)S(1)}) fusion(bf16[1,128,1024]{2,1,0:T(8,128)(2,1)} %param.5), kind=kLoop, calls=%fused_computation | loop fusion | bytes 524288 | tf_op jit(solution)/shard_map/slice | solution.py:97
  5.5 2.7 %collective-permute-start.3 = (bf16[64,1024]{1,0:T(8,128)(2,1)S(1)}, bf16[64,1024]{1,0:T(8,128)(2,1)S(1)}, u32[]{:S(2)}, u32[]{:S(2)}) collective-permute-start(bf16[64,1024]{1,0:T(8,128)(2,1)S(1)} %get-tuple-element.14.refs_5_), channel_id=1, source_target_pairs={{0,4},{4,0},{1,5},{5,1},{2,6},{6,2},{3,7},{7,3},{8,12},{12,8},{9,1... | collective-permute-start | bytes 393224 | tf_op jit(solution)/shard_map/ppermute | solution.py:96
  8.2 0.2 collective-permute-start.4
  8.4 0.8 %select_reduce_fusion = s32[4]{0:T(128)S(1)} fusion(s32[4]{0:T(128)} %param.8), kind=kLoop, calls=%fused_computation.2 | loop fusion | flops 44 | bytes 32 | tf_op jit(solution)/shard_map/reduce_sum | solution.py:102
  9.2 0.6 %broadcast_xor_fusion = (s32[4]{0:T(128)S(1)}, s32[]{:T(128)}) fusion(s32[4]{0:T(128)S(1)} %select_reduce_fusion, s32[]{:T(128)S(6)} %add.15, s32[]{:T(128)S(6)} %axis_index.43), kind=kLoop, calls=%fused_computation.10 | loop fusion | flops 15 | bytes 44 | tf_op jit(solution)/shard_map/xor | solution.py:103
  9.8 3.9 %collective-permute-done.1.refs_2_ = bf16[128,1024]{1,0:T(8,128)(2,1)S(1)} collective-permute-done((bf16[128,1024]{1,0:T(8,128)(2,1)}, bf16[128,1024]{1,0:T(8,128)(2,1)S(1)}, u32[]{:S(2)}, u32[]{:S(2)}) %collective-permute-start.1) | collective-permute-done | bytes 262176 | tf_op jit(solution)/shard_map/ppermute | solution.py:92
  13.7 0.2 collective-permute-start.2
  14.0 0.1 pad_add_fusion.place_ref
  14.7 0.0 collective-permute-done.refs_1_
  14.7 0.0 copy-start
  14.8 0.9 %copy-done = bf16[1,128,1024]{2,1,0:T(8,128)(2,1)S(1)} copy-done((bf16[1,128,1024]{2,1,0:T(8,128)(2,1)S(1)}, bf16[1,128,1024]{2,1,0:T(8,128)(2,1)}, u32[]{:S(2)}) %copy-start) | copy-done | bytes 262168
  15.7 0.0 copy-start.1
  15.7 1.6 %copy-done.1 = bf16[1,1024,1024]{2,1,0:T(8,128)(2,1)S(1)} copy-done((bf16[1,1024,1024]{2,1,0:T(8,128)(2,1)S(1)}, bf16[1,1024,1024]{2,1,0:T(8,128)(2,1)}, u32[]{:S(2)}) %copy-start.1) | copy-done | bytes 2097176
  17.3 2.0 %shard_map.55 = (bf16[1024,1024]{1,0:T(8,128)(2,1)S(1)}, bf16[128,1024]{1,0:T(8,128)(2,1)S(1)}, bf16[128,1024]{1,0:T(8,128)(2,1)S(1)}, bf16[128,1024]{1,0:T(8,128)(2,1)S(1)}) custom-call(s32[1]{0:T(128)S(6)} %copy.6.live_ref, bf16[1024,1024]{1,0:T(8,128)(2,1)S(1)} %bitcast.14, bf16[128,1024]{1,0:T(8,128)(2,1)S(1)} %bitcast.13, ...), custom_call_target="tpu_custom_call" | custom-call | flops 809500672 | bytes 5767168 | tf_op jit(solution)/shard_map/pallas_call | solution.py:112
  19.3 0.0 collective-permute-done.3.refs_7_
  19.3 0.0 collective-permute-done.4.refs_8_
  19.3 0.8 %collective-permute-done.2.refs_3_ = bf16[128,1024]{1,0:T(8,128)(2,1)S(1)} collective-permute-done((bf16[128,1024]{1,0:T(8,128)(2,1)S(1)}, bf16[128,1024]{1,0:T(8,128)(2,1)S(1)}, u32[]{:S(2)}, u32[]{:S(2)}) %collective-permute-start.2) | collective-permute-done | bytes 262176 | tf_op jit(solution)/shard_map/ppermute | solution.py:99
  20.1 2.4 %shard_map.56 = bf16[4,4,64,128]{3,2,1,0:T(8,128)(2,1)} custom-call(s32[8]{0:T(128)S(1)} %pad_add_fusion.place_ref, bf16[128,1024]{1,0:T(8,128)(2,1)S(1)} %get-tuple-element.9.refs_0_, bf16[128,1024]{1,0:T(8,128)(2,1)S(1)} %get-tuple-element.10.refs_1_, bf16[128,1024]{1,0:T(8,128)(2,1)S(1)} %get-tuple-element.11.refs_2_, ...), custom_call_target="tpu_custom_call" | custom-call | flops 536870912 | bytes 4194304 | tf_op jit(solution)/shard_map/pallas_call | solution.py:127
  22.5 3.5 %all-to-all-start = ((bf16[16,64,128]{2,1,0:T(8,128)(2,1)}), bf16[16,64,128]{2,1,0:T(8,128)(2,1)S(1)}, u32[]{:S(2)}, u32[]{:S(2)}) async-start(bf16[16,64,128]{2,1,0:T(8,128)(2,1)} %bitcast.5), calls=%async_computation | async-start | bytes 524288 | tf_op jit(solution)/shard_map/all_to_all | solution.py:144
  26.6 6.5 %all-to-all-done = bf16[16,64,128]{2,1,0:T(8,128)(2,1)S(1)} async-done(((bf16[16,64,128]{2,1,0:T(8,128)(2,1)}), bf16[16,64,128]{2,1,0:T(8,128)(2,1)S(1)}, u32[]{:S(2)}, u32[]{:S(2)}) %all-to-all-start) | async-done | bytes 262176 | tf_op jit(solution)/shard_map/all_to_all | solution.py:144
  33.1 0.8 %shard_map.57 = bf16[4,128,256]{2,1,0:T(8,128)(2,1)} custom-call(s32[1]{0:T(128)} %bitcast.swap_ref, bf16[4,4,64,128]{3,2,1,0:T(8,128)(2,1)S(1)} %bitcast.10), custom_call_target="tpu_custom_call" | custom-call | tf_op jit(solution)/shard_map/pallas_call | solution.py:146
  (2 shorter events, 0.0 us)
Async XLA Ops:
  0.0 14.7 %collective-permute-start = (bf16[128,1024]{1,0:T(8,128)(2,1)}, bf16[128,1024]{1,0:T(8,128)(2,1)S(1)}, u32[]{:S(2)}, u32[]{:S(2)}) collective-permute-start(bf16[128,1024]{1,0:T(8,128)(2,1)} %bitcast.11), channel_id=1, source_target_pairs={{0,1},{1,0},{2,3},{3,2},{4,5},{5,4},{6,7},{7,6},{8,9},{9,8},{10,11... | collective-permute-start | bytes 786440 | tf_op jit(solution)/shard_map/ppermute | solution.py:93
  3.0 10.8 %collective-permute-start.1 = (bf16[128,1024]{1,0:T(8,128)(2,1)}, bf16[128,1024]{1,0:T(8,128)(2,1)S(1)}, u32[]{:S(2)}, u32[]{:S(2)}) collective-permute-start(bf16[128,1024]{1,0:T(8,128)(2,1)} %bitcast.12), channel_id=1, source_target_pairs={{0,2},{2,0},{1,3},{3,1},{4,6},{6,4},{5,7},{7,5},{8,10},{10,8},{9,1... | collective-permute-start | bytes 786440 | tf_op jit(solution)/shard_map/ppermute | solution.py:92
  5.5 13.8 %collective-permute-start.3 = (bf16[64,1024]{1,0:T(8,128)(2,1)S(1)}, bf16[64,1024]{1,0:T(8,128)(2,1)S(1)}, u32[]{:S(2)}, u32[]{:S(2)}) collective-permute-start(bf16[64,1024]{1,0:T(8,128)(2,1)S(1)} %get-tuple-element.14.refs_5_), channel_id=1, source_target_pairs={{0,4},{4,0},{1,5},{5,1},{2,6},{6,2},{3,7},{7,3},{8,12},{12,8},{9,1... | collective-permute-start | bytes 393224 | tf_op jit(solution)/shard_map/ppermute | solution.py:96
  8.2 11.1 %collective-permute-start.4 = (bf16[64,1024]{1,0:T(8,128)(2,1)S(1)}, bf16[64,1024]{1,0:T(8,128)(2,1)S(1)}, u32[]{:S(2)}, u32[]{:S(2)}) collective-permute-start(bf16[64,1024]{1,0:T(8,128)(2,1)S(1)} %get-tuple-element.13), channel_id=1, source_target_pairs={{0,6},{2,4},{4,2},{6,0},{1,7},{3,5},{5,3},{7,1},{8,14},{10,12},{12... | collective-permute-start | bytes 393224 | tf_op jit(solution)/shard_map/ppermute | solution.py:97
  13.7 6.4 %collective-permute-start.2 = (bf16[128,1024]{1,0:T(8,128)(2,1)S(1)}, bf16[128,1024]{1,0:T(8,128)(2,1)S(1)}, u32[]{:S(2)}, u32[]{:S(2)}) collective-permute-start(bf16[128,1024]{1,0:T(8,128)(2,1)S(1)} %collective-permute-done.1.refs_2_), channel_id=1, source_target_pairs={{0,1},{1,0},{2,3},{3,2},{4,5},{5,4},{6,7},{7,6},{8,9},{9,8},{10,11... | collective-permute-start | bytes 786440 | tf_op jit(solution)/shard_map/ppermute | solution.py:99
  14.7 1.0 %copy-start = (bf16[1,128,1024]{2,1,0:T(8,128)(2,1)S(1)}, bf16[1,128,1024]{2,1,0:T(8,128)(2,1)}, u32[]{:S(2)}) copy-start(bf16[1,128,1024]{2,1,0:T(8,128)(2,1)} %param.5) | copy-start | bytes 786436
  15.7 1.6 %copy-start.1 = (bf16[1,1024,1024]{2,1,0:T(8,128)(2,1)S(1)}, bf16[1,1024,1024]{2,1,0:T(8,128)(2,1)}, u32[]{:S(2)}) copy-start(bf16[1,1024,1024]{2,1,0:T(8,128)(2,1)} %param.6) | copy-start | bytes 6291460
  22.5 10.6 %all-to-all-start = ((bf16[16,64,128]{2,1,0:T(8,128)(2,1)}), bf16[16,64,128]{2,1,0:T(8,128)(2,1)S(1)}, u32[]{:S(2)}, u32[]{:S(2)}) async-start(bf16[16,64,128]{2,1,0:T(8,128)(2,1)} %bitcast.5), calls=%async_computation | async-start | bytes 524288 | tf_op jit(solution)/shard_map/all_to_all | solution.py:144

commit v2 on v1

v2 whole, which is shorter than its diff:
```python
import functools

import jax
import jax.numpy as jnp
from jax import lax
from jax.experimental import pallas as pl
from jax.experimental.pallas import tpu as pltpu
from jax.sharding import Mesh, PartitionSpec as P

F32 = jnp.float32
BF16 = jnp.bfloat16
VMEM_LIMIT = 48 * 1024 * 1024
WEIGHT = 10**11


def dot_nt(a, b):
    return lax.dot_general(a, b, (((1,), (1,)), ((), ())), preferred_element_type=F32)


def first_kernel(live_ref, v_ref, *refs):
    n_rows = (len(refs) - 1) // 2
    t_refs, vm_ref, w_refs = refs[:n_rows], refs[n_rows], refs[n_rows + 1 :]
    width = v_ref.shape[0]
    tile = min(256, width)
    live = live_ref[0]
    for i in range(0, width, tile):
        row_live = lax.broadcasted_iota(jnp.int32, (tile, tile), 0) + i < live
        for j in range(0, width, tile):
            col_live = lax.broadcasted_iota(jnp.int32, (tile, tile), 1) + j < live
            here = v_ref[i : i + tile, j : j + tile].astype(F32)
            there = v_ref[j : j + tile, i : i + tile].astype(F32)
            mean = (here + there.T) * 0.5
            vm_ref[i : i + tile, j : j + tile] = jnp.where(row_live & col_live, mean, 0.0).astype(BF16)
    for t_ref, w_ref in zip(t_refs, w_refs):
        w_ref[...] = jnp.dot(t_ref[...], vm_ref[...], preferred_element_type=F32).astype(BF16)


def tiles_kernel(n_w, n_t, half, owner_ref, *refs):
    w_refs, t_refs, vm_ref = refs[:n_w], refs[n_w : n_w + n_t], refs[n_w + n_t]
    near_ref, h_refs, (out_ref, left, picked) = refs[n_w + n_t + 1], refs[n_w + n_t + 2 : -3], refs[-3:]
    groups = len(h_refs) + 1
    rows = w_refs[0].shape[0]
    plane, line = lax.axis_index("zg") * 2 + lax.axis_index("zp"), lax.axis_index("y")
    ny = lax.axis_size("y")
    of_near = near_ref.at[pl.ds(pl.multiple_of((plane % 2) * half, half), half), :]
    for k, h_ref in enumerate([h_refs[0], of_near, *h_refs[1:]]):
        d = owner_ref[plane ^ k]
        picked[pl.ds(pl.multiple_of(d * half, half), half), :] = h_ref[...]
    for k, w_ref in enumerate(w_refs):
        left[k * rows : (k + 1) * rows, :] = w_ref[...]
    for k, t_ref in enumerate(t_refs):
        w = jnp.dot(t_ref[...], vm_ref[...], preferred_element_type=F32)
        left[(n_w + k) * rows : (n_w + k + 1) * rows, :] = w.astype(BF16)
    first = lax.broadcasted_iota(jnp.int32, (rows // 2, 2 * half), 1) < half
    step = min(4 * half, groups * half)
    for at in range(0, groups * half, step):
        both = dot_nt(left[...], picked[at : at + step, :])
        for k in range(n_w + n_t):
            place = ((plane % 2) ^ (k // ny)) * ny + (line ^ (k % ny))
            for pair in range(step // (2 * half)):
                part = both[k * rows : (k + 1) * rows, pair * 2 * half : (pair + 1) * 2 * half]
                top, bottom = part[: rows // 2], part[rows // 2 :]
                even = jnp.where(first, top, pltpu.roll(bottom, half, 1))
                odd = jnp.where(first, pltpu.roll(top, half, 1), bottom)
                slot = at // half + 2 * pair
                out_ref[slot, place] = even.astype(BF16)
                out_ref[slot + 1, place] = odd.astype(BF16)


def place_kernel(ny, half, in_ref, out_ref, placed, sems):
    channels = in_ref.shape[0]
    deep = in_ref.shape[2]
    first = lax.broadcasted_iota(jnp.int32, (deep, 2 * half), 1) < half
    copies = []
    for c in range(channels):
        for y in range(ny):
            a, b = in_ref[c, y].astype(F32), in_ref[c, ny + y].astype(F32)
            top = jnp.where(first, a, pltpu.roll(b, half, 1))
            bottom = jnp.where(first, pltpu.roll(a, half, 1), b)
            placed[c, :deep, y * 2 * half : (y + 1) * 2 * half] = top.astype(BF16)
            placed[c, deep:, y * 2 * half : (y + 1) * 2 * half] = bottom.astype(BF16)
        copies.append(pltpu.make_async_copy(placed.at[c], out_ref.at[c], sems.at[c]))
        copies[-1].start()
    for copy in copies:
        copy.wait()


def xor_pairs(size, k):
    return [(i, i ^ k) for i in range(size)]


def call(kernel, out_shape, operands, scratch=(), scalars=0, out_space=pltpu.VMEM):
    outs = out_shape if isinstance(out_shape, list) else [out_shape]
    out_spec = pl.BlockSpec(memory_space=out_space)
    return pl.pallas_call(
        kernel,
        out_shape=out_shape,
        in_specs=[pl.BlockSpec(memory_space=pltpu.SMEM)] * scalars
        + [pl.BlockSpec(memory_space=pltpu.VMEM)] * (len(operands) - scalars),
        out_specs=[out_spec] * len(outs) if isinstance(out_shape, list) else out_spec,
        scratch_shapes=list(scratch),
        compiler_params=pltpu.CompilerParams(vmem_limit_bytes=VMEM_LIMIT),
        cost_estimate=pl.CostEstimate(flops=WEIGHT, bytes_accessed=WEIGHT, transcendentals=0),
    )(*operands)


def per_device(t_matrix, v_jacobi, channel_dims, owner_map):
    t, v = t_matrix[0], v_jacobi[0]
    rows, width = t.shape
    half = rows // 2
    groups, nzg, ny = lax.axis_size("chan"), lax.axis_size("zg"), lax.axis_size("y")
    block = jax.ShapeDtypeStruct((rows, width), BF16)

    parity = lax.axis_index("zp")
    near = lax.ppermute(t, "zp", xor_pairs(2, 1))
    side = [lax.ppermute(t, "y", xor_pairs(ny, k)) for k in range(1, ny)]
    same = lax.dynamic_slice_in_dim(t, parity * half, half)
    other = lax.dynamic_slice_in_dim(t, (1 - parity) * half, half)
    shares = [same]
    for k in range(1, nzg):
        shares.append(lax.ppermute(same, "zg", xor_pairs(nzg, k)))
        shares.append(lax.ppermute(other, ("zg", "zp"), xor_pairs(2 * nzg, 2 * k + 1)))
    cross = [lax.ppermute(near, "y", xor_pairs(ny, k)) for k in range(1, ny)]

    early = side + [near]
    made = call(
        first_kernel,
        [jax.ShapeDtypeStruct((width, width), BF16)] + [block] * (1 + len(early)),
        [channel_dims, v, t] + early,
        scalars=1,
    )
    vm, lefts = made[0], list(made[1:])
    tiles = call(
        functools.partial(tiles_kernel, len(lefts), len(cross), half),
        jax.ShapeDtypeStruct((groups, 2 * ny, rows // 2, 2 * half), BF16),
        [owner_map] + lefts + cross + [vm, near] + shares,
        scratch=[pltpu.VMEM((2 * ny * rows, width), BF16), pltpu.VMEM((groups * half, width), BF16)],
        scalars=1,
    )
    sent = tiles.reshape(groups * 2 * ny, rows // 2, 2 * half)
    got = lax.all_to_all(sent, ("chan", "zp", "y"), split_axis=0, concat_axis=0, tiled=True)
    got = got.reshape(groups, 2 * ny, rows // 2, 2 * half)
    out = call(
        functools.partial(place_kernel, ny, half),
        jax.ShapeDtypeStruct((groups, rows, ny * rows), BF16),
        [got],
        scratch=[pltpu.VMEM((groups, rows, ny * rows), BF16), pltpu.SemaphoreType.DMA((groups,))],
        out_space=pl.ANY,
    )
    return out[None]


def solution(mesh):
    chan, blk = mesh.shape["chan"], mesh.shape["blk"]

    def whole(t_matrix, v_jacobi, channel_dims, owner_map):
        block_cols = t_matrix.shape[1] // chan
        ny = block_cols * blk // t_matrix.shape[1]
        inner = Mesh(mesh.devices.reshape(chan, blk // (2 * ny), 2, ny), ("chan", "zg", "zp", "y"))
        line = ("zg", "zp", "y")
        return jax.shard_map(
            per_device,
            mesh=inner,
            in_specs=(P("chan", line, None), P("chan", None, None), P("chan"), P()),
            out_specs=P("chan", None, line, None),
            check_vma=False,
        )(t_matrix, v_jacobi, channel_dims, owner_map)

    return whole
```

time: 34.6 us -> 32.3 us (0.934); the launches traced: 34 us -> 32.1 us
  blocking collectives: 0 us -> 11 us
  waiting for transfers between devices: 11.3 us -> 2.63 us
  other arithmetic: 1.48 us -> 0 us
  starting transfers between devices: 11.2 us -> 9.95 us
  Pallas kernels: 5.21 us -> 4.29 us
  between operations: 1.28 us -> 0.69 us
    all_to_all x0 -> x1, blocking collectives: none -> 11 us  [per_device(): lax.all_to_all(sent, ('chan', 'zp', 'y'), split_axis=0, concat_axis=0, ti...]
    all_to_all x1 -> x0, waiting for transfers between devices: 6.54 us -> none  [per_device(): lax.all_to_all(sent, ('chan', 'zp', 'y'), split_axis=0, concat_axis=0, ti...]
    all_to_all x1 -> x0, starting transfers between devices: 3.53 us -> none  [per_device(): lax.all_to_all(sent, ('chan', 'zp', 'y'), split_axis=0, concat_axis=0, ti...]
    ppermute x1, starting transfers between devices: 0.24 us -> 2.53 us  [per_device(): cross = [lax.ppermute(near, 'y', xor_pairs(ny, k)) for k in range(1, ny)]]
    ppermute x1, waiting for transfers between devices: 3.92 us -> 2.29 us  [per_device(): near = lax.ppermute(t, 'zp', xor_pairs(2, 1))]
    ppermute x1, starting transfers between devices: 2.97 us -> 1.52 us  [per_device(): side = [lax.ppermute(t, 'y', xor_pairs(ny, k)) for k in range(1, ny)]]
    ppermute x1, starting transfers between devices: 1.58 us -> 3.02 us  [per_device(): near = lax.ppermute(t, 'zp', xor_pairs(2, 1))]
    slice x2 -> x0, local copies, waits for them, and re-layouts: 1 us -> none  [the longest x1 0.99 us: per_device(): t[half:]]
  transfers between devices with their start and end apart: 6 -> 5, of which waited for: 3 -> 2; matrix products, arithmetic and copies ran while one was open for 7% -> 3% of each run, Pallas kernels for 6% -> 6%
where the time goes in v2:
time: 32.3 us; the launch traced here: 32.1 us
  blocking collectives  11 us (34%)
  starting transfers between devices  9.95 us (31%)
  Pallas kernels  4.29 us (13%)
  local copies, waits for them, and re-layouts  3.54 us (11%)
  waiting for transfers between devices  2.63 us (8%)
  between operations  0.69 us (2%)
    all_to_all x1, blocking collectives, per_device(): lax.all_to_all(sent, ('chan', 'zp', 'y'), split_axis=0, concat_axis=0, ti...  11 us
    pallas_call x3, Pallas kernels, call(): pl.pallas_call(kernel, out_shape=out_shape, in_specs=[pl.BlockSpec(memory...  4.29 us
    ppermute x1, starting transfers between devices, per_device(): near = lax.ppermute(t, 'zp', xor_pairs(2, 1))  3.02 us
    ppermute x1, starting transfers between devices, per_device(): shares.append(lax.ppermute(same, 'zg', xor_pairs(nzg, k)))  2.65 us
    unnamed x6, local copies, waits for them, and re-layouts  2.54 us
    ppermute x1, starting transfers between devices, per_device(): cross = [lax.ppermute(near, 'y', xor_pairs(ny, k)) for k in range(1, ny)]  2.53 us
    ppermute x1, waiting for transfers between devices, per_device(): near = lax.ppermute(t, 'zp', xor_pairs(2, 1))  2.29 us
    ppermute x1, starting transfers between devices, per_device(): side = [lax.ppermute(t, 'y', xor_pairs(ny, k)) for k in range(1, ny)]  1.52 us
  transfers between devices with their start and end apart: 5, of which 2 were waited for; matrix products, arithmetic and copies ran while one was open for 3% of the time, Pallas kernels for 6%

profile of v2, /device:TPU:0, one launch (start us, length us, event | category | flops | bytes accessed | tf_op | source)
XLA Modules:
  0.0 32.1 jit_solution(4470314549757880510)
XLA Ops:
  0.0 3.0 %collective-permute-start.1 = (bf16[128,1024]{1,0:T(8,128)(2,1)}, bf16[128,1024]{1,0:T(8,128)(2,1)S(1)}, u32[]{:S(2)}, u32[]{:S(2)}) collective-permute-start(bf16[128,1024]{1,0:T(8,128)(2,1)} %bitcast.9), channel_id=1, source_target_pairs={{0,2},{2,0},{1,3},{3,1},{4,6},{6,4},{5,7},{7,5},{8,10},{10,8},{9,1... | collective-permute-start | bytes 786440 | tf_op jit(solution)/shard_map/ppermute | solution.py:115
  3.0 1.5 %collective-permute-start = (bf16[128,1024]{1,0:T(8,128)(2,1)}, bf16[128,1024]{1,0:T(8,128)(2,1)S(1)}, u32[]{:S(2)}, u32[]{:S(2)}) collective-permute-start(bf16[128,1024]{1,0:T(8,128)(2,1)} %bitcast.10), channel_id=1, source_target_pairs={{0,1},{1,0},{2,3},{3,2},{4,5},{5,4},{6,7},{7,6},{8,9},{9,8},{10,11... | collective-permute-start | bytes 786440 | tf_op jit(solution)/shard_map/ppermute | solution.py:116
  4.5 1.0 %dynamic-slice_bitcast_fusion = (bf16[64,1024]{1,0:T(8,128)(2,1)S(1)}, bf16[64,1024]{1,0:T(8,128)(2,1)S(1)}) fusion(bf16[1,128,1024]{2,1,0:T(8,128)(2,1)} %param.4, s32[]{:T(128)S(6)} %select_n.7, s32[]{:T(128)S(6)} %select_n.6), kind=kLoop, calls=%fused_computation | loop fusion | bytes 524296 | tf_op jit(solution)/shard_map/dynamic_slice | solution.py:118
  5.5 2.7 %collective-permute-start.3 = (bf16[64,1024]{1,0:T(8,128)(2,1)S(1)}, bf16[64,1024]{1,0:T(8,128)(2,1)S(1)}, u32[]{:S(2)}, u32[]{:S(2)}) collective-permute-start(bf16[64,1024]{1,0:T(8,128)(2,1)S(1)} %get-tuple-element.14.refs_6_), channel_id=1, source_target_pairs={{0,4},{4,0},{1,5},{5,1},{2,6},{6,2},{3,7},{7,3},{8,12},{12,8},{9,1... | collective-permute-start | bytes 393224 | tf_op jit(solution)/shard_map/ppermute | solution.py:121
  8.2 0.2 collective-permute-start.4
  9.1 2.3 %collective-permute-done.1.refs_2_.refs_5_ = bf16[128,1024]{1,0:T(8,128)(2,1)S(1)} collective-permute-done((bf16[128,1024]{1,0:T(8,128)(2,1)}, bf16[128,1024]{1,0:T(8,128)(2,1)S(1)}, u32[]{:S(2)}, u32[]{:S(2)}) %collective-permute-start.1) | collective-permute-done | bytes 262176 | tf_op jit(solution)/shard_map/ppermute | solution.py:115
  11.4 2.5 %collective-permute-start.2 = (bf16[128,1024]{1,0:T(8,128)(2,1)S(1)}, bf16[128,1024]{1,0:T(8,128)(2,1)S(1)}, u32[]{:S(2)}, u32[]{:S(2)}) collective-permute-start(bf16[128,1024]{1,0:T(8,128)(2,1)S(1)} %collective-permute-done.1.refs_2_.refs_5_), channel_id=1, source_target_pairs={{0,1},{1,0},{2,3},{3,2},{4,5},{5,4},{6,7},{7,6},{8,9},{9,8},{10,11... | collective-permute-start | bytes 786440 | tf_op jit(solution)/shard_map/ppermute | solution.py:123
  13.9 0.0 collective-permute-done.refs_1_
  13.9 0.0 copy-start
  13.9 0.9 %copy-done = bf16[1,128,1024]{2,1,0:T(8,128)(2,1)S(1)} copy-done((bf16[1,128,1024]{2,1,0:T(8,128)(2,1)S(1)}, bf16[1,128,1024]{2,1,0:T(8,128)(2,1)}, u32[]{:S(2)}) %copy-start) | copy-done | bytes 262168
  14.8 0.0 copy-start.1
  14.8 1.6 %copy-done.1 = bf16[1,1024,1024]{2,1,0:T(8,128)(2,1)S(1)} copy-done((bf16[1,1024,1024]{2,1,0:T(8,128)(2,1)S(1)}, bf16[1,1024,1024]{2,1,0:T(8,128)(2,1)}, u32[]{:S(2)}) %copy-start.1) | copy-done | bytes 2097176
  16.4 0.0 copy-start.2
  16.4 2.0 %shard_map.46 = (bf16[1024,1024]{1,0:T(8,128)(2,1)S(1)}, bf16[128,1024]{1,0:T(8,128)(2,1)S(1)}, bf16[128,1024]{1,0:T(8,128)(2,1)S(1)}, bf16[128,1024]{1,0:T(8,128)(2,1)S(1)}) custom-call(s32[1]{0:T(128)S(6)} %copy.5.live_ref, bf16[1024,1024]{1,0:T(8,128)(2,1)S(1)} %bitcast.14, bf16[128,1024]{1,0:T(8,128)(2,1)S(1)} %bitcast.11, ...), custom_call_target="tpu_custom_call" | custom-call | flops 99999997952 | bytes 99999997952 | tf_op jit(solution)/shard_map/pallas_call | solution.py:95
  18.5 0.0 collective-permute-done.3.refs_7_
  18.5 0.0 collective-permute-done.4.refs_8_
  18.5 0.3 %collective-permute-done.2.refs_3_ = bf16[128,1024]{1,0:T(8,128)(2,1)S(1)} collective-permute-done((bf16[128,1024]{1,0:T(8,128)(2,1)S(1)}, bf16[128,1024]{1,0:T(8,128)(2,1)S(1)}, u32[]{:S(2)}, u32[]{:S(2)}) %collective-permute-start.2) | collective-permute-done | bytes 262176 | tf_op jit(solution)/shard_map/ppermute | solution.py:123
  18.8 0.0 copy-done.2
  18.8 1.4 %shard_map.47 = bf16[4,4,64,128]{3,2,1,0:T(8,128)(2,1)S(1)} custom-call(s32[4]{0:T(128)S(1)} %copy-done.2, bf16[128,1024]{1,0:T(8,128)(2,1)S(1)} %get-tuple-element.9.refs_0_, bf16[128,1024]{1,0:T(8,128)(2,1)S(1)} %get-tuple-element.10.refs_1_, bf16[128,1024]{1,0:T(8,128)(2,1)S(1)} %get-tuple-element.11.refs_2_, ...), custom_call_target="tpu_custom_call" | custom-call | flops 99999997952 | bytes 99999997952 | tf_op jit(solution)/shard_map/pallas_call | solution.py:95
  20.3 11.0 %all_to_all.5 = bf16[16,64,128]{2,1,0:T(8,128)(2,1)S(1)} all-to-all(bf16[16,64,128]{2,1,0:T(8,128)(2,1)S(1)} %bitcast.12), channel_id=1, replica_groups=mesh['chan'=4,'zg'=2,'zp'=2,'y'=2] {'chan','zp','y'}, dimensions={0} | all-to-all | bytes 524288 | tf_op jit(solution)/shard_map/all_to_all | solution.py:141
  31.3 0.8 %shard_map.48 = bf16[4,128,256]{2,1,0:T(8,128)(2,1)} custom-call(bf16[4,4,64,128]{3,2,1,0:T(8,128)(2,1)S(1)} %bitcast.13), custom_call_target="tpu_custom_call" | custom-call | flops 99999997952 | bytes 99999997952 | tf_op jit(solution)/shard_map/pallas_call | solution.py:95
Async XLA Ops:
  0.0 11.4 %collective-permute-start.1 = (bf16[128,1024]{1,0:T(8,128)(2,1)}, bf16[128,1024]{1,0:T(8,128)(2,1)S(1)}, u32[]{:S(2)}, u32[]{:S(2)}) collective-permute-start(bf16[128,1024]{1,0:T(8,128)(2,1)} %bitcast.9), channel_id=1, source_target_pairs={{0,2},{2,0},{1,3},{3,1},{4,6},{6,4},{5,7},{7,5},{8,10},{10,8},{9,1... | collective-permute-start | bytes 786440 | tf_op jit(solution)/shard_map/ppermute | solution.py:115
  3.0 10.9 %collective-permute-start = (bf16[128,1024]{1,0:T(8,128)(2,1)}, bf16[128,1024]{1,0:T(8,128)(2,1)S(1)}, u32[]{:S(2)}, u32[]{:S(2)}) collective-permute-start(bf16[128,1024]{1,0:T(8,128)(2,1)} %bitcast.10), channel_id=1, source_target_pairs={{0,1},{1,0},{2,3},{3,2},{4,5},{5,4},{6,7},{7,6},{8,9},{9,8},{10,11... | collective-permute-start | bytes 786440 | tf_op jit(solution)/shard_map/ppermute | solution.py:116
  5.5 12.9 %collective-permute-start.3 = (bf16[64,1024]{1,0:T(8,128)(2,1)S(1)}, bf16[64,1024]{1,0:T(8,128)(2,1)S(1)}, u32[]{:S(2)}, u32[]{:S(2)}) collective-permute-start(bf16[64,1024]{1,0:T(8,128)(2,1)S(1)} %get-tuple-element.14.refs_6_), channel_id=1, source_target_pairs={{0,4},{4,0},{1,5},{5,1},{2,6},{6,2},{3,7},{7,3},{8,12},{12,8},{9,1... | collective-permute-start | bytes 393224 | tf_op jit(solution)/shard_map/ppermute | solution.py:121
  8.2 10.3 %collective-permute-start.4 = (bf16[64,1024]{1,0:T(8,128)(2,1)S(1)}, bf16[64,1024]{1,0:T(8,128)(2,1)S(1)}, u32[]{:S(2)}, u32[]{:S(2)}) collective-permute-start(bf16[64,1024]{1,0:T(8,128)(2,1)S(1)} %get-tuple-element.13), channel_id=1, source_target_pairs={{0,6},{2,4},{4,2},{6,0},{1,7},{3,5},{5,3},{7,1},{8,14},{10,12},{12... | collective-permute-start | bytes 393224 | tf_op jit(solution)/shard_map/ppermute | solution.py:122
  11.4 7.5 %collective-permute-start.2 = (bf16[128,1024]{1,0:T(8,128)(2,1)S(1)}, bf16[128,1024]{1,0:T(8,128)(2,1)S(1)}, u32[]{:S(2)}, u32[]{:S(2)}) collective-permute-start(bf16[128,1024]{1,0:T(8,128)(2,1)S(1)} %collective-permute-done.1.refs_2_.refs_5_), channel_id=1, source_target_pairs={{0,1},{1,0},{2,3},{3,2},{4,5},{5,4},{6,7},{7,6},{8,9},{9,8},{10,11... | collective-permute-start | bytes 786440 | tf_op jit(solution)/shard_map/ppermute | solution.py:123
  13.9 1.0 %copy-start = (bf16[1,128,1024]{2,1,0:T(8,128)(2,1)S(1)}, bf16[1,128,1024]{2,1,0:T(8,128)(2,1)}, u32[]{:S(2)}) copy-start(bf16[1,128,1024]{2,1,0:T(8,128)(2,1)} %param.4) | copy-start | bytes 786436
  14.8 1.6 %copy-start.1 = (bf16[1,1024,1024]{2,1,0:T(8,128)(2,1)S(1)}, bf16[1,1024,1024]{2,1,0:T(8,128)(2,1)}, u32[]{:S(2)}) copy-start(bf16[1,1024,1024]{2,1,0:T(8,128)(2,1)} %param.5) | copy-start | bytes 6291460
  16.4 2.4 %copy-start.2 = (s32[4]{0:T(128)S(1)}, s32[4]{0:T(128)}, u32[]{:S(2)}) copy-start(s32[4]{0:T(128)} %owner_ref.1) | copy-start | bytes 52

commit v3 on v2

--- a/solution.py
+++ b/solution.py
@@ -18,8 +18,7 @@
 
 
 def first_kernel(live_ref, v_ref, *refs):
-    n_rows = (len(refs) - 1) // 2
-    t_refs, vm_ref, w_refs = refs[:n_rows], refs[n_rows], refs[n_rows + 1 :]
+    t_refs, (vm_ref, w_ref) = refs[:-2], refs[-2:]
     width = v_ref.shape[0]
     tile = min(256, width)
     live = live_ref[0]
@@ -31,40 +30,45 @@
             there = v_ref[j : j + tile, i : i + tile].astype(F32)
             mean = (here + there.T) * 0.5
             vm_ref[i : i + tile, j : j + tile] = jnp.where(row_live & col_live, mean, 0.0).astype(BF16)
-    for t_ref, w_ref in zip(t_refs, w_refs):
-        w_ref[...] = jnp.dot(t_ref[...], vm_ref[...], preferred_element_type=F32).astype(BF16)
+    rows = t_refs[0].shape[0]
+    for k, t_ref in enumerate(t_refs):
+        w = jnp.dot(t_ref[...], vm_ref[...], preferred_element_type=F32)
+        w_ref[k * rows : (k + 1) * rows, :] = w.astype(BF16)
 
 
-def tiles_kernel(n_w, n_t, half, owner_ref, *refs):
-    w_refs, t_refs, vm_ref = refs[:n_w], refs[n_w : n_w + n_t], refs[n_w + n_t]
-    near_ref, h_refs, (out_ref, left, picked) = refs[n_w + n_t + 1], refs[n_w + n_t + 2 : -3], refs[-3:]
-    groups = len(h_refs) + 1
-    rows = w_refs[0].shape[0]
-    plane, line = lax.axis_index("zg") * 2 + lax.axis_index("zp"), lax.axis_index("y")
-    ny = lax.axis_size("y")
-    of_near = near_ref.at[pl.ds(pl.multiple_of((plane % 2) * half, half), half), :]
+def tiles_kernel(half, owner_ref, w_ref, vm_ref, near_ref, *refs):
+    zg, zp, line = lax.axis_index("zg"), lax.axis_index("zp"), lax.axis_index("y")
+    plane, ny = zg * 2 + zp, lax.axis_size("y")
+    groups = 2 * lax.axis_size("zg")
+    cross_refs, h_refs, (out_ref, picked) = refs[: ny - 1], refs[ny - 1 : -2], refs[-2:]
+    rows = near_ref.shape[0]
+    of_near = near_ref.at[pl.ds(pl.multiple_of(zp * half, half), half), :]
     for k, h_ref in enumerate([h_refs[0], of_near, *h_refs[1:]]):
-        d = owner_ref[plane ^ k]
+        d = jnp.sum(jnp.where(lax.broadcasted_iota(jnp.int32, owner_ref.shape, 1) == (plane ^ k), owner_ref[...], 0))
         picked[pl.ds(pl.multiple_of(d * half, half), half), :] = h_ref[...]
-    for k, w_ref in enumerate(w_refs):
-        left[k * rows : (k + 1) * rows, :] = w_ref[...]
-    for k, t_ref in enumerate(t_refs):
-        w = jnp.dot(t_ref[...], vm_ref[...], preferred_element_type=F32)
-        left[(n_w + k) * rows : (n_w + k + 1) * rows, :] = w.astype(BF16)
     first = lax.broadcasted_iota(jnp.int32, (rows // 2, 2 * half), 1) < half
     step = min(4 * half, groups * half)
-    for at in range(0, groups * half, step):
-        both = dot_nt(left[...], picked[at : at + step, :])
-        for k in range(n_w + n_t):
-            place = ((plane % 2) ^ (k // ny)) * ny + (line ^ (k % ny))
-            for pair in range(step // (2 * half)):
-                part = both[k * rows : (k + 1) * rows, pair * 2 * half : (pair + 1) * 2 * half]
-                top, bottom = part[: rows // 2], part[rows // 2 :]
-                even = jnp.where(first, top, pltpu.roll(bottom, half, 1))
-                odd = jnp.where(first, pltpu.roll(top, half, 1), bottom)
-                slot = at // half + 2 * pair
-                out_ref[slot, place] = even.astype(BF16)
-                out_ref[slot + 1, place] = odd.astype(BF16)
+
+    def tiles(left, k_first):
+        for at in range(0, groups * half, step):
+            both = dot_nt(left, picked[at : at + step, :])
+            for i in range(left.shape[0] // rows):
+                k = k_first + i
+                place = (zp ^ (k // ny)) * ny + (line ^ (k % ny))
+                for pair in range(step // (2 * half)):
+                    part = both[i * rows : (i + 1) * rows, pair * 2 * half : (pair + 1) * 2 * half]
+                    top, bottom = part[: rows // 2], part[rows // 2 :]
+                    even = jnp.where(first, top, pltpu.roll(bottom, half, 1))
+                    odd = jnp.where(first, pltpu.roll(top, half, 1), bottom)
+                    slot = at // half + 2 * pair
+                    out_ref[slot, place] = even.astype(BF16)
+                    out_ref[slot + 1, place] = odd.astype(BF16)
+
+    ws = []
+    for k, t_ref in enumerate(cross_refs):
+        w = jnp.dot(t_ref[...], vm_ref[...], preferred_element_type=F32).astype(BF16)
+        ws.append(w)
+    tiles(jnp.concatenate([w_ref[...]] + ws, axis=0), 0)
 
 
 def place_kernel(ny, half, in_ref, out_ref, placed, sems):
@@ -104,13 +108,10 @@
     )(*operands)
 
 
-def per_device(t_matrix, v_jacobi, channel_dims, owner_map):
-    t, v = t_matrix[0], v_jacobi[0]
+def lab_tiles(t, v, channel_dims, owner_map):
     rows, width = t.shape
     half = rows // 2
     groups, nzg, ny = lax.axis_size("chan"), lax.axis_size("zg"), lax.axis_size("y")
-    block = jax.ShapeDtypeStruct((rows, width), BF16)
-
     parity = lax.axis_index("zp")
     near = lax.ppermute(t, "zp", xor_pairs(2, 1))
     side = [lax.ppermute(t, "y", xor_pairs(ny, k)) for k in range(1, ny)]
@@ -122,21 +123,28 @@
         shares.append(lax.ppermute(other, ("zg", "zp"), xor_pairs(2 * nzg, 2 * k + 1)))
     cross = [lax.ppermute(near, "y", xor_pairs(ny, k)) for k in range(1, ny)]
 
-    early = side + [near]
-    made = call(
+    lefts = [t] + side + [near]
+    vm, w = call(
         first_kernel,
-        [jax.ShapeDtypeStruct((width, width), BF16)] + [block] * (1 + len(early)),
-        [channel_dims, v, t] + early,
+        [jax.ShapeDtypeStruct((width, width), BF16), jax.ShapeDtypeStruct((len(lefts) * rows, width), BF16)],
+        [channel_dims, v] + lefts,
         scalars=1,
     )
-    vm, lefts = made[0], list(made[1:])
-    tiles = call(
-        functools.partial(tiles_kernel, len(lefts), len(cross), half),
+    return call(
+        functools.partial(tiles_kernel, half),
         jax.ShapeDtypeStruct((groups, 2 * ny, rows // 2, 2 * half), BF16),
-        [owner_map] + lefts + cross + [vm, near] + shares,
-        scratch=[pltpu.VMEM((2 * ny * rows, width), BF16), pltpu.VMEM((groups * half, width), BF16)],
-        scalars=1,
+        [owner_map[None, :], w, vm, near] + cross + shares,
+        scratch=[pltpu.VMEM((groups * half, width), BF16)],
     )
+
+
+def per_device(t_matrix, v_jacobi, channel_dims, owner_map):
+    t, v = t_matrix[0], v_jacobi[0]
+    rows = t.shape[0]
+    half = rows // 2
+    groups, ny = lax.axis_size("chan"), lax.axis_size("y")
+    tiles = lab_tiles(t, v, channel_dims, owner_map)
+
     sent = tiles.reshape(groups * 2 * ny, rows // 2, 2 * half)
     got = lax.all_to_all(sent, ("chan", "zp", "y"), split_axis=0, concat_axis=0, tiled=True)
     got = got.reshape(groups, 2 * ny, rows // 2, 2 * half)

time: 32.3 us -> 31.8 us (0.985)
  Pallas kernels: 4.29 us -> 3.75 us
    pallas_call x3, Pallas kernels: 4.29 us -> 3.75 us  [call(): pl.pallas_call(kernel, out_shape=out_shape, in_specs=[pl.BlockSpec(memory...]
where the time goes in v3:
time: 31.8 us; the launch traced here: 31.6 us
  blocking collectives  11 us (35%)
  starting transfers between devices  9.95 us (31%)
  Pallas kernels  3.75 us (12%)
  local copies, waits for them, and re-layouts  3.54 us (11%)
  waiting for transfers between devices  2.63 us (8%)
  between operations  0.69 us (2%)
    all_to_all x1, blocking collectives, per_device(): lax.all_to_all(sent, ('chan', 'zp', 'y'), split_axis=0, concat_axis=0, ti...  11 us
    pallas_call x3, Pallas kernels, call(): pl.pallas_call(kernel, out_shape=out_shape, in_specs=[pl.BlockSpec(memory...  3.75 us
    ppermute x1, starting transfers between devices, lab_tiles(): near = lax.ppermute(t, 'zp', xor_pairs(2, 1))  3.02 us
    ppermute x1, starting transfers between devices, lab_tiles(): shares.append(lax.ppermute(same, 'zg', xor_pairs(nzg, k)))  2.65 us
    unnamed x6, local copies, waits for them, and re-layouts  2.54 us
    ppermute x1, starting transfers between devices, lab_tiles(): cross = [lax.ppermute(near, 'y', xor_pairs(ny, k)) for k in range(1, ny)]  2.53 us
    ppermute x1, waiting for transfers between devices, lab_tiles(): near = lax.ppermute(t, 'zp', xor_pairs(2, 1))  2.29 us
    ppermute x1, starting transfers between devices, lab_tiles(): side = [lax.ppermute(t, 'y', xor_pairs(ny, k)) for k in range(1, ny)]  1.52 us
  transfers between devices with their start and end apart: 5, of which 2 were waited for; matrix products, arithmetic and copies ran while one was open for 3% of the time, Pallas kernels for 6%

profile of v3, /device:TPU:0, one launch (start us, length us, event | category | flops | bytes accessed | tf_op | source)
XLA Modules:
  0.0 31.6 jit_solution(921554563654270168)
XLA Ops:
  0.0 3.0 %collective-permute-start.1 = (bf16[128,1024]{1,0:T(8,128)(2,1)}, bf16[128,1024]{1,0:T(8,128)(2,1)S(1)}, u32[]{:S(2)}, u32[]{:S(2)}) collective-permute-start(bf16[128,1024]{1,0:T(8,128)(2,1)} %bitcast.10), channel_id=1, source_target_pairs={{0,2},{2,0},{1,3},{3,1},{4,6},{6,4},{5,7},{7,5},{8,10},{10,8},{9,1... | collective-permute-start | bytes 786440 | tf_op jit(solution)/shard_map/ppermute | solution.py:116
  3.0 1.5 %collective-permute-start = (bf16[128,1024]{1,0:T(8,128)(2,1)}, bf16[128,1024]{1,0:T(8,128)(2,1)S(1)}, u32[]{:S(2)}, u32[]{:S(2)}) collective-permute-start(bf16[128,1024]{1,0:T(8,128)(2,1)} %bitcast.11), channel_id=1, source_target_pairs={{0,1},{1,0},{2,3},{3,2},{4,5},{5,4},{6,7},{7,6},{8,9},{9,8},{10,11... | collective-permute-start | bytes 786440 | tf_op jit(solution)/shard_map/ppermute | solution.py:117
  4.5 1.0 %dynamic-slice_bitcast_fusion = (bf16[64,1024]{1,0:T(8,128)(2,1)S(1)}, bf16[64,1024]{1,0:T(8,128)(2,1)S(1)}) fusion(bf16[1,128,1024]{2,1,0:T(8,128)(2,1)} %param.4, s32[]{:T(128)S(6)} %select_n.7, s32[]{:T(128)S(6)} %select_n.6), kind=kLoop, calls=%fused_computation | loop fusion | bytes 524296 | tf_op jit(solution)/shard_map/dynamic_slice | solution.py:119
  5.5 2.7 %collective-permute-start.3 = (bf16[64,1024]{1,0:T(8,128)(2,1)S(1)}, bf16[64,1024]{1,0:T(8,128)(2,1)S(1)}, u32[]{:S(2)}, u32[]{:S(2)}) collective-permute-start(bf16[64,1024]{1,0:T(8,128)(2,1)S(1)} %get-tuple-element.10.refs_1_), channel_id=1, source_target_pairs={{0,4},{4,0},{1,5},{5,1},{2,6},{6,2},{3,7},{7,3},{8,12},{12,8},{9,1... | collective-permute-start | bytes 393224 | tf_op jit(solution)/shard_map/ppermute | solution.py:122
  8.2 0.2 collective-permute-start.4
  9.1 2.3 %collective-permute-done.1.refs_2_.near_ref = bf16[128,1024]{1,0:T(8,128)(2,1)S(1)} collective-permute-done((bf16[128,1024]{1,0:T(8,128)(2,1)}, bf16[128,1024]{1,0:T(8,128)(2,1)S(1)}, u32[]{:S(2)}, u32[]{:S(2)}) %collective-permute-start.1) | collective-permute-done | bytes 262176 | tf_op jit(solution)/shard_map/ppermute | solution.py:116
  11.4 2.5 %collective-permute-start.2 = (bf16[128,1024]{1,0:T(8,128)(2,1)S(1)}, bf16[128,1024]{1,0:T(8,128)(2,1)S(1)}, u32[]{:S(2)}, u32[]{:S(2)}) collective-permute-start(bf16[128,1024]{1,0:T(8,128)(2,1)S(1)} %collective-permute-done.1.refs_2_.near_ref), channel_id=1, source_target_pairs={{0,1},{1,0},{2,3},{3,2},{4,5},{5,4},{6,7},{7,6},{8,9},{9,8},{10,11... | collective-permute-start | bytes 786440 | tf_op jit(solution)/shard_map/ppermute | solution.py:124
  13.9 0.0 collective-permute-done.refs_1_
  13.9 0.0 copy-start
  13.9 0.9 %copy-done = bf16[1,128,1024]{2,1,0:T(8,128)(2,1)S(1)} copy-done((bf16[1,128,1024]{2,1,0:T(8,128)(2,1)S(1)}, bf16[1,128,1024]{2,1,0:T(8,128)(2,1)}, u32[]{:S(2)}) %copy-start) | copy-done | bytes 262168
  14.8 0.0 copy-start.1
  14.8 1.6 %copy-done.1 = bf16[1,1024,1024]{2,1,0:T(8,128)(2,1)S(1)} copy-done((bf16[1,1024,1024]{2,1,0:T(8,128)(2,1)S(1)}, bf16[1,1024,1024]{2,1,0:T(8,128)(2,1)}, u32[]{:S(2)}) %copy-start.1) | copy-done | bytes 2097176
  16.4 0.0 copy-start.2
  16.4 2.0 %shard_map.46 = (bf16[1024,1024]{1,0:T(8,128)(2,1)S(1)}, bf16[384,1024]{1,0:T(8,128)(2,1)S(1)}) custom-call(s32[1]{0:T(128)S(6)} %copy.5.live_ref, bf16[1024,1024]{1,0:T(8,128)(2,1)S(1)} %bitcast.15, bf16[128,1024]{1,0:T(8,128)(2,1)S(1)} %bitcast.12, bf16[128,1024]{1,0:T(8,128)(2,1)S(1)} %collective-permute-done.refs_1_, ...), custom_call_target="tpu_custom_call" | custom-call | flops 99999997952 | bytes 99999997952 | tf_op jit(solution)/shard_map/pallas_call | solution.py:99
  18.5 0.0 collective-permute-done.3.refs_2_
  18.5 0.0 collective-permute-done.4.refs_3_
  18.5 0.3 %collective-permute-done.2.refs_0_ = bf16[128,1024]{1,0:T(8,128)(2,1)S(1)} collective-permute-done((bf16[128,1024]{1,0:T(8,128)(2,1)S(1)}, bf16[128,1024]{1,0:T(8,128)(2,1)S(1)}, u32[]{:S(2)}, u32[]{:S(2)}) %collective-permute-start.2) | collective-permute-done | bytes 262176 | tf_op jit(solution)/shard_map/ppermute | solution.py:124
  18.8 0.0 copy-done.2
  18.8 0.9 %shard_map.47 = bf16[4,4,64,128]{3,2,1,0:T(8,128)(2,1)S(1)} custom-call(s32[1,4]{1,0:T(1,128)S(1)} %bitcast.16, bf16[384,1024]{1,0:T(8,128)(2,1)S(1)} %get-tuple-element.7.w_ref, bf16[1024,1024]{1,0:T(8,128)(2,1)S(1)} %get-tuple-element.8.vm_ref, bf16[128,1024]{1,0:T(8,128)(2,1)S(1)} %collective-permute-done.1.refs_2_.near_ref, ...), custom_call_target="tpu_custom_call" | custom-call | flops 99999997952 | bytes 99999997952 | tf_op jit(solution)/shard_map/pallas_call | solution.py:99
  19.7 11.0 %all_to_all.5 = bf16[16,64,128]{2,1,0:T(8,128)(2,1)S(1)} all-to-all(bf16[16,64,128]{2,1,0:T(8,128)(2,1)S(1)} %bitcast.13), channel_id=1, replica_groups=mesh['chan'=4,'zg'=2,'zp'=2,'y'=2] {'chan','zp','y'}, dimensions={0} | all-to-all | bytes 524288 | tf_op jit(solution)/shard_map/all_to_all | solution.py:149
  30.8 0.8 %shard_map.48 = bf16[4,128,256]{2,1,0:T(8,128)(2,1)} custom-call(bf16[4,4,64,128]{3,2,1,0:T(8,128)(2,1)S(1)} %bitcast.14), custom_call_target="tpu_custom_call" | custom-call | flops 99999997952 | bytes 99999997952 | tf_op jit(solution)/shard_map/pallas_call | solution.py:99
Async XLA Ops:
  0.0 11.4 %collective-permute-start.1 = (bf16[128,1024]{1,0:T(8,128)(2,1)}, bf16[128,1024]{1,0:T(8,128)(2,1)S(1)}, u32[]{:S(2)}, u32[]{:S(2)}) collective-permute-start(bf16[128,1024]{1,0:T(8,128)(2,1)} %bitcast.10), channel_id=1, source_target_pairs={{0,2},{2,0},{1,3},{3,1},{4,6},{6,4},{5,7},{7,5},{8,10},{10,8},{9,1... | collective-permute-start | bytes 786440 | tf_op jit(solution)/shard_map/ppermute | solution.py:116
  3.0 10.9 %collective-permute-start = (bf16[128,1024]{1,0:T(8,128)(2,1)}, bf16[128,1024]{1,0:T(8,128)(2,1)S(1)}, u32[]{:S(2)}, u32[]{:S(2)}) collective-permute-start(bf16[128,1024]{1,0:T(8,128)(2,1)} %bitcast.11), channel_id=1, source_target_pairs={{0,1},{1,0},{2,3},{3,2},{4,5},{5,4},{6,7},{7,6},{8,9},{9,8},{10,11... | collective-permute-start | bytes 786440 | tf_op jit(solution)/shard_map/ppermute | solution.py:117
  5.5 12.9 %collective-permute-start.3 = (bf16[64,1024]{1,0:T(8,128)(2,1)S(1)}, bf16[64,1024]{1,0:T(8,128)(2,1)S(1)}, u32[]{:S(2)}, u32[]{:S(2)}) collective-permute-start(bf16[64,1024]{1,0:T(8,128)(2,1)S(1)} %get-tuple-element.10.refs_1_), channel_id=1, source_target_pairs={{0,4},{4,0},{1,5},{5,1},{2,6},{6,2},{3,7},{7,3},{8,12},{12,8},{9,1... | collective-permute-start | bytes 393224 | tf_op jit(solution)/shard_map/ppermute | solution.py:122
  8.2 10.3 %collective-permute-start.4 = (bf16[64,1024]{1,0:T(8,128)(2,1)S(1)}, bf16[64,1024]{1,0:T(8,128)(2,1)S(1)}, u32[]{:S(2)}, u32[]{:S(2)}) collective-permute-start(bf16[64,1024]{1,0:T(8,128)(2,1)S(1)} %get-tuple-element.9), channel_id=1, source_target_pairs={{0,6},{2,4},{4,2},{6,0},{1,7},{3,5},{5,3},{7,1},{8,14},{10,12},{12... | collective-permute-start | bytes 393224 | tf_op jit(solution)/shard_map/ppermute | solution.py:123
  11.4 7.5 %collective-permute-start.2 = (bf16[128,1024]{1,0:T(8,128)(2,1)S(1)}, bf16[128,1024]{1,0:T(8,128)(2,1)S(1)}, u32[]{:S(2)}, u32[]{:S(2)}) collective-permute-start(bf16[128,1024]{1,0:T(8,128)(2,1)S(1)} %collective-permute-done.1.refs_2_.near_ref), channel_id=1, source_target_pairs={{0,1},{1,0},{2,3},{3,2},{4,5},{5,4},{6,7},{7,6},{8,9},{9,8},{10,11... | collective-permute-start | bytes 786440 | tf_op jit(solution)/shard_map/ppermute | solution.py:124
  13.9 1.0 %copy-start = (bf16[1,128,1024]{2,1,0:T(8,128)(2,1)S(1)}, bf16[1,128,1024]{2,1,0:T(8,128)(2,1)}, u32[]{:S(2)}) copy-start(bf16[1,128,1024]{2,1,0:T(8,128)(2,1)} %param.4) | copy-start | bytes 786436
  14.8 1.6 %copy-start.1 = (bf16[1,1024,1024]{2,1,0:T(8,128)(2,1)S(1)}, bf16[1,1024,1024]{2,1,0:T(8,128)(2,1)}, u32[]{:S(2)}) copy-start(bf16[1,1024,1024]{2,1,0:T(8,128)(2,1)} %param.5) | copy-start | bytes 6291460
  16.4 2.4 %copy-start.2 = (s32[4]{0:T(128)S(1)}, s32[4]{0:T(128)}, u32[]{:S(2)}) copy-start(s32[4]{0:T(128)} %param.7) | copy-start | bytes 52

commit v4 on v3

--- a/solution.py
+++ b/solution.py
@@ -15,6 +15,11 @@
 
 def dot_nt(a, b):
     return lax.dot_general(a, b, (((1,), (1,)), ((), ())), preferred_element_type=F32)
+
+
+def order_kernel(in_ref, out_ref):
+    plane = lax.axis_index("zg") * 2 + lax.axis_index("zp")
+    out_ref[...] = in_ref[...] ^ plane
 
 
 def first_kernel(live_ref, v_ref, *refs):
@@ -36,7 +41,7 @@
         w_ref[k * rows : (k + 1) * rows, :] = w.astype(BF16)
 
 
-def tiles_kernel(half, owner_ref, w_ref, vm_ref, near_ref, *refs):
+def tiles_kernel(half, order_ref, owner_ref, w_ref, vm_ref, near_ref, *refs):
     zg, zp, line = lax.axis_index("zg"), lax.axis_index("zp"), lax.axis_index("y")
     plane, ny = zg * 2 + zp, lax.axis_size("y")
     groups = 2 * lax.axis_size("zg")
@@ -44,7 +49,7 @@
     rows = near_ref.shape[0]
     of_near = near_ref.at[pl.ds(pl.multiple_of(zp * half, half), half), :]
     for k, h_ref in enumerate([h_refs[0], of_near, *h_refs[1:]]):
-        d = jnp.sum(jnp.where(lax.broadcasted_iota(jnp.int32, owner_ref.shape, 1) == (plane ^ k), owner_ref[...], 0))
+        d = jnp.sum(jnp.where(order_ref[...] == k, owner_ref[...], 0))
         picked[pl.ds(pl.multiple_of(d * half, half), half), :] = h_ref[...]
     first = lax.broadcasted_iota(jnp.int32, (rows // 2, 2 * half), 1) < half
     step = min(4 * half, groups * half)
@@ -93,7 +98,17 @@
     return [(i, i ^ k) for i in range(size)]
 
 
-def call(kernel, out_shape, operands, scratch=(), scalars=0, out_space=pltpu.VMEM):
+def turn_pairs(channels, ny, k):
+    pairs = []
+    for c in range(channels):
+        for p in range(2):
+            for y in range(ny):
+                to = (1 - p) * ny + y if c % 2 else p * ny + (y ^ k)
+                pairs.append(((2 * c + p) * ny + y, 2 * c * ny + to))
+    return pairs
+
+
+def call(kernel, out_shape, operands, scratch=(), scalars=0, out_space=pltpu.VMEM, weight=WEIGHT):
     outs = out_shape if isinstance(out_shape, list) else [out_shape]
     out_spec = pl.BlockSpec(memory_space=out_space)
     return pl.pallas_call(
@@ -104,7 +119,7 @@
         out_specs=[out_spec] * len(outs) if isinstance(out_shape, list) else out_spec,
         scratch_shapes=list(scratch),
         compiler_params=pltpu.CompilerParams(vmem_limit_bytes=VMEM_LIMIT),
-        cost_estimate=pl.CostEstimate(flops=WEIGHT, bytes_accessed=WEIGHT, transcendentals=0),
+        cost_estimate=pl.CostEstimate(flops=weight, bytes_accessed=weight, transcendentals=0),
     )(*operands)
 
 
@@ -121,7 +136,14 @@
     for k in range(1, nzg):
         shares.append(lax.ppermute(same, "zg", xor_pairs(nzg, k)))
         shares.append(lax.ppermute(other, ("zg", "zp"), xor_pairs(2 * nzg, 2 * k + 1)))
-    cross = [lax.ppermute(near, "y", xor_pairs(ny, k)) for k in range(1, ny)]
+    odd = lax.axis_index("chan") % 2 > 0
+    planes, near = lax.optimization_barrier((jnp.arange(groups, dtype=jnp.int32)[None, :], near))
+    order = call(order_kernel, jax.ShapeDtypeStruct((1, groups), jnp.int32), [planes], weight=1)
+    near, order = lax.optimization_barrier((near, order))
+    cross = [
+        lax.ppermute(jnp.where(odd, other_line, near), ("chan", "zp", "y"), turn_pairs(groups, ny, k))
+        for k, other_line in enumerate(side, 1)
+    ]
 
     lefts = [t] + side + [near]
     vm, w = call(
@@ -133,7 +155,7 @@
     return call(
         functools.partial(tiles_kernel, half),
         jax.ShapeDtypeStruct((groups, 2 * ny, rows // 2, 2 * half), BF16),
-        [owner_map[None, :], w, vm, near] + cross + shares,
+        [order, owner_map[None, :], w, vm, near] + cross + shares,
         scratch=[pltpu.VMEM((groups * half, width), BF16)],
     )
 

time: 31.8 us -> 31.6 us (level)
  waiting for transfers between devices: 2.63 us -> 2.29 us
    ppermute x1, waiting for transfers between devices: 0.33 us -> 0.01 us  [lab_tiles(): lax.ppermute(jnp.where(odd, other_line, near), ('chan', 'zp', 'y'), turn_...]
    pallas_call x3 -> x4, Pallas kernels: 3.75 us -> 3.72 us  [call(): pl.pallas_call(kernel, out_shape=out_shape, in_specs=[pl.BlockSpec(memory...]
  transfers between devices with their start and end apart: 5 -> 5, of which waited for: 2 -> 1; matrix products, arithmetic and copies ran while one was open for 3% -> 3% of each run, Pallas kernels for 6% -> 6%
where the time goes in v4:
time: 31.6 us; the launch traced here: 31.4 us
  blocking collectives  11 us (35%)
  starting transfers between devices  10 us (32%)
  Pallas kernels  3.72 us (12%)
  local copies, waits for them, and re-layouts  3.54 us (11%)
  waiting for transfers between devices  2.29 us (7%)
  between operations  0.72 us (2%)
    all_to_all x1, blocking collectives, per_device(): lax.all_to_all(sent, ('chan', 'zp', 'y'), split_axis=0, concat_axis=0, ti...  11 us
    pallas_call x4, Pallas kernels, call(): pl.pallas_call(kernel, out_shape=out_shape, in_specs=[pl.BlockSpec(memory...  3.72 us
    ppermute x1, starting transfers between devices, lab_tiles(): near = lax.ppermute(t, 'zp', xor_pairs(2, 1))  3.02 us
    ppermute x1, starting transfers between devices, lab_tiles(): shares.append(lax.ppermute(same, 'zg', xor_pairs(nzg, k)))  2.65 us
    ppermute x1, starting transfers between devices, lab_tiles(): lax.ppermute(jnp.where(odd, other_line, near), ('chan', 'zp', 'y'), turn_...  2.6 us
    unnamed x6, local copies, waits for them, and re-layouts  2.54 us
    ppermute x1, waiting for transfers between devices, lab_tiles(): near = lax.ppermute(t, 'zp', xor_pairs(2, 1))  2.28 us
    ppermute x1, starting transfers between devices, lab_tiles(): side = [lax.ppermute(t, 'y', xor_pairs(ny, k)) for k in range(1, ny)]  1.52 us
  transfers between devices with their start and end apart: 5, of which 1 were waited for; matrix products, arithmetic and copies ran while one was open for 3% of the time, Pallas kernels for 6%

profile of v4, /device:TPU:0, one launch (start us, length us, event | category | flops | bytes accessed | tf_op | source)
XLA Modules:
  0.0 31.4 jit_solution(8402248633644697472)
XLA Ops:
  0.0 3.0 %collective-permute-start = (bf16[128,1024]{1,0:T(8,128)(2,1)}, bf16[128,1024]{1,0:T(8,128)(2,1)S(1)}, u32[]{:S(2)}, u32[]{:S(2)}) collective-permute-start(bf16[128,1024]{1,0:T(8,128)(2,1)} %bitcast.10), channel_id=1, source_target_pairs={{0,2},{2,0},{1,3},{3,1},{4,6},{6,4},{5,7},{7,5},{8,10},{10,8},{9,1... | collective-permute-start | bytes 786440 | tf_op jit(solution)/shard_map/ppermute | solution.py:131
  3.0 1.5 %collective-permute-start.1 = (bf16[128,1024]{1,0:T(8,128)(2,1)}, bf16[128,1024]{1,0:T(8,128)(2,1)S(1)}, u32[]{:S(2)}, u32[]{:S(2)}) collective-permute-start(bf16[128,1024]{1,0:T(8,128)(2,1)} %bitcast.11), channel_id=1, source_target_pairs={{0,1},{1,0},{2,3},{3,2},{4,5},{5,4},{6,7},{7,6},{8,9},{9,8},{10,11... | collective-permute-start | bytes 786440 | tf_op jit(solution)/shard_map/ppermute | solution.py:132
  4.5 1.0 %dynamic-slice_bitcast_fusion = (bf16[64,1024]{1,0:T(8,128)(2,1)S(1)}, bf16[64,1024]{1,0:T(8,128)(2,1)S(1)}) fusion(bf16[1,128,1024]{2,1,0:T(8,128)(2,1)} %param.4, s32[]{:T(128)S(6)} %select_n.25, s32[]{:T(128)S(6)} %select_n.24), kind=kLoop, calls=%fused_computation.1 | loop fusion | bytes 524296 | tf_op jit(solution)/shard_map/dynamic_slice | solution.py:134
  5.5 2.7 %collective-permute-start.3 = (bf16[64,1024]{1,0:T(8,128)(2,1)S(1)}, bf16[64,1024]{1,0:T(8,128)(2,1)S(1)}, u32[]{:S(2)}, u32[]{:S(2)}) collective-permute-start(bf16[64,1024]{1,0:T(8,128)(2,1)S(1)} %get-tuple-element.18.refs_1_), channel_id=1, source_target_pairs={{0,4},{4,0},{1,5},{5,1},{2,6},{6,2},{3,7},{7,3},{8,12},{12,8},{9,1... | collective-permute-start | bytes 393224 | tf_op jit(solution)/shard_map/ppermute | solution.py:137
  8.2 0.2 collective-permute-start.4
  9.1 2.3 %collective-permute-done.refs_2_.near_ref = bf16[128,1024]{1,0:T(8,128)(2,1)S(1)} collective-permute-done((bf16[128,1024]{1,0:T(8,128)(2,1)}, bf16[128,1024]{1,0:T(8,128)(2,1)S(1)}, u32[]{:S(2)}, u32[]{:S(2)}) %collective-permute-start) | collective-permute-done | bytes 262176 | tf_op jit(solution)/shard_map/ppermute | solution.py:131
  11.4 0.0 collective-permute-done.1.refs_1_
  11.4 2.6 %collective-permute-start.2 = (bf16[128,1024]{1,0:T(8,128)(2,1)S(1)}, bf16[128,1024]{1,0:T(8,128)(2,1)S(1)}, u32[]{:S(2)}, u32[]{:S(2)}) collective-permute-start(bf16[128,1024]{1,0:T(8,128)(2,1)S(1)} %broadcast_select_fusion), channel_id=1, source_target_pairs={{0,1},{1,0},{2,3},{3,2},{8,10},{9,11},{10,8},{11,9},{16,17},{17,16... | collective-permute-start | bytes 786440 | tf_op jit(solution)/shard_map/ppermute | solution.py:144
  14.0 0.0 copy-start
  14.0 0.9 %copy-done = bf16[1,128,1024]{2,1,0:T(8,128)(2,1)S(1)} copy-done((bf16[1,128,1024]{2,1,0:T(8,128)(2,1)S(1)}, bf16[1,128,1024]{2,1,0:T(8,128)(2,1)}, u32[]{:S(2)}) %copy-start) | copy-done | bytes 262168
  15.0 0.0 copy-start.1
  15.0 1.6 %copy-done.1 = bf16[1,1024,1024]{2,1,0:T(8,128)(2,1)S(1)} copy-done((bf16[1,1024,1024]{2,1,0:T(8,128)(2,1)S(1)}, bf16[1,1024,1024]{2,1,0:T(8,128)(2,1)}, u32[]{:S(2)}) %copy-start.1) | copy-done | bytes 2097176
  16.5 0.0 copy-start.2
  16.6 2.0 %shard_map.47 = (bf16[1024,1024]{1,0:T(8,128)(2,1)S(1)}, bf16[384,1024]{1,0:T(8,128)(2,1)S(1)}) custom-call(s32[1]{0:T(128)S(6)} %copy.5.live_ref, bf16[1024,1024]{1,0:T(8,128)(2,1)S(1)} %bitcast.15, bf16[128,1024]{1,0:T(8,128)(2,1)S(1)} %bitcast.12, bf16[128,1024]{1,0:T(8,128)(2,1)S(1)} %collective-permute-done.1.refs_1_, ...), custom_call_target="tpu_custom_call" | custom-call | flops 99999997952 | bytes 99999997952 | tf_op jit(solution)/shard_map/pallas_call | solution.py:114
  18.6 0.0 collective-permute-done.3.refs_2_
  18.6 0.0 collective-permute-done.4.refs_3_
  18.6 0.0 collective-permute-done.2.refs_0_
  18.6 0.0 copy-done.2
  18.6 0.9 %shard_map.48 = bf16[4,4,64,128]{3,2,1,0:T(8,128)(2,1)S(1)} custom-call(s32[1,4]{1,0:T(1,128)S(1)} %shard_map.46.order_ref, s32[1,4]{1,0:T(1,128)S(1)} %bitcast.16, bf16[384,1024]{1,0:T(8,128)(2,1)S(1)} %get-tuple-element.15.w_ref, bf16[1024,1024]{1,0:T(8,128)(2,1)S(1)} %get-tuple-element.16.vm_ref, ...), custom_call_target="tpu_custom_call" | custom-call | flops 99999997952 | bytes 99999997952 | tf_op jit(solution)/shard_map/pallas_call | solution.py:114
  19.5 11.0 %all_to_all.5 = bf16[16,64,128]{2,1,0:T(8,128)(2,1)S(1)} all-to-all(bf16[16,64,128]{2,1,0:T(8,128)(2,1)S(1)} %bitcast.13), channel_id=1, replica_groups=mesh['chan'=4,'zg'=2,'zp'=2,'y'=2] {'chan','zp','y'}, dimensions={0} | all-to-all | bytes 524288 | tf_op jit(solution)/shard_map/all_to_all | solution.py:171
  30.5 0.8 %shard_map.49 = bf16[4,128,256]{2,1,0:T(8,128)(2,1)} custom-call(bf16[4,4,64,128]{3,2,1,0:T(8,128)(2,1)S(1)} %bitcast.14), custom_call_target="tpu_custom_call" | custom-call | flops 99999997952 | bytes 99999997952 | tf_op jit(solution)/shard_map/pallas_call | solution.py:114
  (3 shorter events, 0.0 us)
Async XLA Ops:
  0.0 11.4 %collective-permute-start = (bf16[128,1024]{1,0:T(8,128)(2,1)}, bf16[128,1024]{1,0:T(8,128)(2,1)S(1)}, u32[]{:S(2)}, u32[]{:S(2)}) collective-permute-start(bf16[128,1024]{1,0:T(8,128)(2,1)} %bitcast.10), channel_id=1, source_target_pairs={{0,2},{2,0},{1,3},{3,1},{4,6},{6,4},{5,7},{7,5},{8,10},{10,8},{9,1... | collective-permute-start | bytes 786440 | tf_op jit(solution)/shard_map/ppermute | solution.py:131
  3.0 8.3 %collective-permute-start.1 = (bf16[128,1024]{1,0:T(8,128)(2,1)}, bf16[128,1024]{1,0:T(8,128)(2,1)S(1)}, u32[]{:S(2)}, u32[]{:S(2)}) collective-permute-start(bf16[128,1024]{1,0:T(8,128)(2,1)} %bitcast.11), channel_id=1, source_target_pairs={{0,1},{1,0},{2,3},{3,2},{4,5},{5,4},{6,7},{7,6},{8,9},{9,8},{10,11... | collective-permute-start | bytes 786440 | tf_op jit(solution)/shard_map/ppermute | solution.py:132
  5.5 13.0 %collective-permute-start.3 = (bf16[64,1024]{1,0:T(8,128)(2,1)S(1)}, bf16[64,1024]{1,0:T(8,128)(2,1)S(1)}, u32[]{:S(2)}, u32[]{:S(2)}) collective-permute-start(bf16[64,1024]{1,0:T(8,128)(2,1)S(1)} %get-tuple-element.18.refs_1_), channel_id=1, source_target_pairs={{0,4},{4,0},{1,5},{5,1},{2,6},{6,2},{3,7},{7,3},{8,12},{12,8},{9,1... | collective-permute-start | bytes 393224 | tf_op jit(solution)/shard_map/ppermute | solution.py:137
  8.2 10.4 %collective-permute-start.4 = (bf16[64,1024]{1,0:T(8,128)(2,1)S(1)}, bf16[64,1024]{1,0:T(8,128)(2,1)S(1)}, u32[]{:S(2)}, u32[]{:S(2)}) collective-permute-start(bf16[64,1024]{1,0:T(8,128)(2,1)S(1)} %get-tuple-element.17), channel_id=1, source_target_pairs={{0,6},{2,4},{4,2},{6,0},{1,7},{3,5},{5,3},{7,1},{8,14},{10,12},{12... | collective-permute-start | bytes 393224 | tf_op jit(solution)/shard_map/ppermute | solution.py:138
  11.4 7.2 %collective-permute-start.2 = (bf16[128,1024]{1,0:T(8,128)(2,1)S(1)}, bf16[128,1024]{1,0:T(8,128)(2,1)S(1)}, u32[]{:S(2)}, u32[]{:S(2)}) collective-permute-start(bf16[128,1024]{1,0:T(8,128)(2,1)S(1)} %broadcast_select_fusion), channel_id=1, source_target_pairs={{0,1},{1,0},{2,3},{3,2},{8,10},{9,11},{10,8},{11,9},{16,17},{17,16... | collective-permute-start | bytes 786440 | tf_op jit(solution)/shard_map/ppermute | solution.py:144
  14.0 0.9 %copy-start = (bf16[1,128,1024]{2,1,0:T(8,128)(2,1)S(1)}, bf16[1,128,1024]{2,1,0:T(8,128)(2,1)}, u32[]{:S(2)}) copy-start(bf16[1,128,1024]{2,1,0:T(8,128)(2,1)} %param.4) | copy-start | bytes 786436
  15.0 1.6 %copy-start.1 = (bf16[1,1024,1024]{2,1,0:T(8,128)(2,1)S(1)}, bf16[1,1024,1024]{2,1,0:T(8,128)(2,1)}, u32[]{:S(2)}) copy-start(bf16[1,1024,1024]{2,1,0:T(8,128)(2,1)} %param.5) | copy-start | bytes 6291460
  16.5 2.0 %copy-start.2 = (s32[4]{0:T(128)S(1)}, s32[4]{0:T(128)}, u32[]{:S(2)}) copy-start(s32[4]{0:T(128)} %param.7) | copy-start | bytes 52

commit v5 on v4

--- a/solution.py
+++ b/solution.py
@@ -138,7 +138,7 @@
         shares.append(lax.ppermute(other, ("zg", "zp"), xor_pairs(2 * nzg, 2 * k + 1)))
     odd = lax.axis_index("chan") % 2 > 0
     planes, near = lax.optimization_barrier((jnp.arange(groups, dtype=jnp.int32)[None, :], near))
-    order = call(order_kernel, jax.ShapeDtypeStruct((1, groups), jnp.int32), [planes], weight=1)
+    order = call(order_kernel, jax.ShapeDtypeStruct((1, groups), jnp.int32), [planes], weight=10**9)
     near, order = lax.optimization_barrier((near, order))
     cross = [
         lax.ppermute(jnp.where(odd, other_line, near), ("chan", "zp", "y"), turn_pairs(groups, ny, k))

time: 31.6 us -> 31.6 us (level)
  local copies, waits for them, and re-layouts: 3.54 us -> 1.01 us
  waiting for transfers between devices: 2.29 us -> 4.77 us
    unnamed x6, local copies, waits for them, and re-layouts: 2.54 us -> 0.01 us
    ppermute x1, waiting for transfers between devices: 0.01 us -> 1.95 us  [lab_tiles(): shares.append(lax.ppermute(same, 'zg', xor_pairs(nzg, k)))]
    ppermute x1, waiting for transfers between devices: 0.01 us -> 0.53 us  [lab_tiles(): lax.ppermute(other, ('zg', 'zp'), xor_pairs(2 * nzg, 2 * k + 1))]
  transfers between devices with their start and end apart: 5 -> 5, of which waited for: 1 -> 3; matrix products, arithmetic and copies ran while one was open for 3% -> 3% of each run, Pallas kernels for 6% -> 6%
where the time goes in v5:
time: 31.6 us; the launch traced here: 31.4 us
  blocking collectives  11.1 us (35%)
  starting transfers between devices  10 us (32%)
  waiting for transfers between devices  4.77 us (15%)
  Pallas kernels  3.73 us (12%)
  local copies, waits for them, and re-layouts  1.01 us (3%)
  between operations  0.71 us (2%)
    all_to_all x1, blocking collectives, per_device(): lax.all_to_all(sent, ('chan', 'zp', 'y'), split_axis=0, concat_axis=0, ti...  11.1 us
    pallas_call x4, Pallas kernels, call(): pl.pallas_call(kernel, out_shape=out_shape, in_specs=[pl.BlockSpec(memory...  3.73 us
    ppermute x1, starting transfers between devices, lab_tiles(): near = lax.ppermute(t, 'zp', xor_pairs(2, 1))  3.02 us
    ppermute x1, starting transfers between devices, lab_tiles(): shares.append(lax.ppermute(same, 'zg', xor_pairs(nzg, k)))  2.65 us
    ppermute x1, starting transfers between devices, lab_tiles(): lax.ppermute(jnp.where(odd, other_line, near), ('chan', 'zp', 'y'), turn_...  2.6 us
    ppermute x1, waiting for transfers between devices, lab_tiles(): near = lax.ppermute(t, 'zp', xor_pairs(2, 1))  2.28 us
    ppermute x1, waiting for transfers between devices, lab_tiles(): shares.append(lax.ppermute(same, 'zg', xor_pairs(nzg, k)))  1.95 us
    ppermute x1, starting transfers between devices, lab_tiles(): side = [lax.ppermute(t, 'y', xor_pairs(ny, k)) for k in range(1, ny)]  1.52 us
  transfers between devices with their start and end apart: 5, of which 3 were waited for; matrix products, arithmetic and copies ran while one was open for 3% of the time, Pallas kernels for 6%

profile of v5, /device:TPU:0, one launch (start us, length us, event | category | flops | bytes accessed | tf_op | source)
XLA Modules:
  0.0 31.4 jit_solution(15654748525072417500)
XLA Ops:
  0.0 3.0 %collective-permute-start = (bf16[128,1024]{1,0:T(8,128)(2,1)}, bf16[128,1024]{1,0:T(8,128)(2,1)S(1)}, u32[]{:S(2)}, u32[]{:S(2)}) collective-permute-start(bf16[128,1024]{1,0:T(8,128)(2,1)} %bitcast.10), channel_id=1, source_target_pairs={{0,2},{2,0},{1,3},{3,1},{4,6},{6,4},{5,7},{7,5},{8,10},{10,8},{9,1... | collective-permute-start | bytes 786440 | tf_op jit(solution)/shard_map/ppermute | solution.py:131
  3.0 1.5 %collective-permute-start.1 = (bf16[128,1024]{1,0:T(8,128)(2,1)}, bf16[128,1024]{1,0:T(8,128)(2,1)S(1)}, u32[]{:S(2)}, u32[]{:S(2)}) collective-permute-start(bf16[128,1024]{1,0:T(8,128)(2,1)} %bitcast.11), channel_id=1, source_target_pairs={{0,1},{1,0},{2,3},{3,2},{4,5},{5,4},{6,7},{7,6},{8,9},{9,8},{10,11... | collective-permute-start | bytes 786440 | tf_op jit(solution)/shard_map/ppermute | solution.py:132
  4.5 1.0 %dynamic-slice_bitcast_fusion = (bf16[64,1024]{1,0:T(8,128)(2,1)S(1)}, bf16[64,1024]{1,0:T(8,128)(2,1)S(1)}) fusion(bf16[1,128,1024]{2,1,0:T(8,128)(2,1)} %param.4, s32[]{:T(128)S(6)} %select_n.25, s32[]{:T(128)S(6)} %select_n.24), kind=kLoop, calls=%fused_computation.1 | loop fusion | bytes 524296 | tf_op jit(solution)/shard_map/dynamic_slice | solution.py:134
  5.5 2.7 %collective-permute-start.3 = (bf16[64,1024]{1,0:T(8,128)(2,1)S(1)}, bf16[64,1024]{1,0:T(8,128)(2,1)S(1)}, u32[]{:S(2)}, u32[]{:S(2)}) collective-permute-start(bf16[64,1024]{1,0:T(8,128)(2,1)S(1)} %get-tuple-element.18.refs_1_), channel_id=1, source_target_pairs={{0,4},{4,0},{1,5},{5,1},{2,6},{6,2},{3,7},{7,3},{8,12},{12,8},{9,1... | collective-permute-start | bytes 393224 | tf_op jit(solution)/shard_map/ppermute | solution.py:137
  8.2 0.2 collective-permute-start.4
  9.1 2.3 %collective-permute-done.refs_2_.near_ref = bf16[128,1024]{1,0:T(8,128)(2,1)S(1)} collective-permute-done((bf16[128,1024]{1,0:T(8,128)(2,1)}, bf16[128,1024]{1,0:T(8,128)(2,1)S(1)}, u32[]{:S(2)}, u32[]{:S(2)}) %collective-permute-start) | collective-permute-done | bytes 262176 | tf_op jit(solution)/shard_map/ppermute | solution.py:131
  11.4 0.0 copy-start
  11.4 0.0 copy-start.1
  11.4 0.0 collective-permute-done.1.refs_1_
  11.4 2.6 %collective-permute-start.2 = (bf16[128,1024]{1,0:T(8,128)(2,1)S(1)}, bf16[128,1024]{1,0:T(8,128)(2,1)S(1)}, u32[]{:S(2)}, u32[]{:S(2)}) collective-permute-start(bf16[128,1024]{1,0:T(8,128)(2,1)S(1)} %broadcast_select_fusion), channel_id=1, source_target_pairs={{0,1},{1,0},{2,3},{3,2},{8,10},{9,11},{10,8},{11,9},{16,17},{17,16... | collective-permute-start | bytes 786440 | tf_op jit(solution)/shard_map/ppermute | solution.py:144
  14.0 0.0 copy-done
  14.0 0.0 copy-done.1
  14.0 0.0 copy-start.2
  14.0 2.0 %shard_map.47 = (bf16[1024,1024]{1,0:T(8,128)(2,1)S(1)}, bf16[384,1024]{1,0:T(8,128)(2,1)S(1)}) custom-call(s32[1]{0:T(128)S(6)} %copy.5.live_ref, bf16[1024,1024]{1,0:T(8,128)(2,1)S(1)} %bitcast.15, bf16[128,1024]{1,0:T(8,128)(2,1)S(1)} %bitcast.12, bf16[128,1024]{1,0:T(8,128)(2,1)S(1)} %collective-permute-done.1.refs_1_, ...), custom_call_target="tpu_custom_call" | custom-call | flops 99999997952 | bytes 99999997952 | tf_op jit(solution)/shard_map/pallas_call | solution.py:114
  16.1 1.9 %collective-permute-done.3.refs_2_ = bf16[64,1024]{1,0:T(8,128)(2,1)S(1)} collective-permute-done((bf16[64,1024]{1,0:T(8,128)(2,1)S(1)}, bf16[64,1024]{1,0:T(8,128)(2,1)S(1)}, u32[]{:S(2)}, u32[]{:S(2)}) %collective-permute-start.3) | collective-permute-done | bytes 131104 | tf_op jit(solution)/shard_map/ppermute | solution.py:137
  18.0 0.5 %collective-permute-done.4.refs_3_ = bf16[64,1024]{1,0:T(8,128)(2,1)S(1)} collective-permute-done((bf16[64,1024]{1,0:T(8,128)(2,1)S(1)}, bf16[64,1024]{1,0:T(8,128)(2,1)S(1)}, u32[]{:S(2)}, u32[]{:S(2)}) %collective-permute-start.4) | collective-permute-done | bytes 131104 | tf_op jit(solution)/shard_map/ppermute | solution.py:138
  18.5 0.0 collective-permute-done.2.refs_0_
  18.5 0.0 copy-done.2
  18.5 0.9 %shard_map.48 = bf16[4,4,64,128]{3,2,1,0:T(8,128)(2,1)S(1)} custom-call(s32[1,4]{1,0:T(1,128)S(1)} %shard_map.46.order_ref, s32[1,4]{1,0:T(1,128)S(1)} %bitcast.16, bf16[384,1024]{1,0:T(8,128)(2,1)S(1)} %get-tuple-element.15.w_ref, bf16[1024,1024]{1,0:T(8,128)(2,1)S(1)} %get-tuple-element.16.vm_ref, ...), custom_call_target="tpu_custom_call" | custom-call | flops 99999997952 | bytes 99999997952 | tf_op jit(solution)/shard_map/pallas_call | solution.py:114
  19.4 11.1 %all_to_all.5 = bf16[16,64,128]{2,1,0:T(8,128)(2,1)S(1)} all-to-all(bf16[16,64,128]{2,1,0:T(8,128)(2,1)S(1)} %bitcast.13), channel_id=1, replica_groups=mesh['chan'=4,'zg'=2,'zp'=2,'y'=2] {'chan','zp','y'}, dimensions={0} | all-to-all | bytes 524288 | tf_op jit(solution)/shard_map/all_to_all | solution.py:171
  30.6 0.8 %shard_map.49 = bf16[4,128,256]{2,1,0:T(8,128)(2,1)} custom-call(bf16[4,4,64,128]{3,2,1,0:T(8,128)(2,1)S(1)} %bitcast.14), custom_call_target="tpu_custom_call" | custom-call | flops 99999997952 | bytes 99999997952 | tf_op jit(solution)/shard_map/pallas_call | solution.py:114
  (3 shorter events, 0.0 us)
Async XLA Ops:
  0.0 11.4 %collective-permute-start = (bf16[128,1024]{1,0:T(8,128)(2,1)}, bf16[128,1024]{1,0:T(8,128)(2,1)S(1)}, u32[]{:S(2)}, u32[]{:S(2)}) collective-permute-start(bf16[128,1024]{1,0:T(8,128)(2,1)} %bitcast.10), channel_id=1, source_target_pairs={{0,2},{2,0},{1,3},{3,1},{4,6},{6,4},{5,7},{7,5},{8,10},{10,8},{9,1... | collective-permute-start | bytes 786440 | tf_op jit(solution)/shard_map/ppermute | solution.py:131
  3.0 8.4 %collective-permute-start.1 = (bf16[128,1024]{1,0:T(8,128)(2,1)}, bf16[128,1024]{1,0:T(8,128)(2,1)S(1)}, u32[]{:S(2)}, u32[]{:S(2)}) collective-permute-start(bf16[128,1024]{1,0:T(8,128)(2,1)} %bitcast.11), channel_id=1, source_target_pairs={{0,1},{1,0},{2,3},{3,2},{4,5},{5,4},{6,7},{7,6},{8,9},{9,8},{10,11... | collective-permute-start | bytes 786440 | tf_op jit(solution)/shard_map/ppermute | solution.py:132
  5.5 12.5 %collective-permute-start.3 = (bf16[64,1024]{1,0:T(8,128)(2,1)S(1)}, bf16[64,1024]{1,0:T(8,128)(2,1)S(1)}, u32[]{:S(2)}, u32[]{:S(2)}) collective-permute-start(bf16[64,1024]{1,0:T(8,128)(2,1)S(1)} %get-tuple-element.18.refs_1_), channel_id=1, source_target_pairs={{0,4},{4,0},{1,5},{5,1},{2,6},{6,2},{3,7},{7,3},{8,12},{12,8},{9,1... | collective-permute-start | bytes 393224 | tf_op jit(solution)/shard_map/ppermute | solution.py:137
  8.2 10.3 %collective-permute-start.4 = (bf16[64,1024]{1,0:T(8,128)(2,1)S(1)}, bf16[64,1024]{1,0:T(8,128)(2,1)S(1)}, u32[]{:S(2)}, u32[]{:S(2)}) collective-permute-start(bf16[64,1024]{1,0:T(8,128)(2,1)S(1)} %get-tuple-element.17), channel_id=1, source_target_pairs={{0,6},{2,4},{4,2},{6,0},{1,7},{3,5},{5,3},{7,1},{8,14},{10,12},{12... | collective-permute-start | bytes 393224 | tf_op jit(solution)/shard_map/ppermute | solution.py:138
  11.4 2.7 %copy-start = (bf16[1,128,1024]{2,1,0:T(8,128)(2,1)S(1)}, bf16[1,128,1024]{2,1,0:T(8,128)(2,1)}, u32[]{:S(2)}) copy-start(bf16[1,128,1024]{2,1,0:T(8,128)(2,1)} %param.4) | copy-start | bytes 786436
  11.4 2.7 %copy-start.1 = (bf16[1,1024,1024]{2,1,0:T(8,128)(2,1)S(1)}, bf16[1,1024,1024]{2,1,0:T(8,128)(2,1)}, u32[]{:S(2)}) copy-start(bf16[1,1024,1024]{2,1,0:T(8,128)(2,1)} %param.5) | copy-start | bytes 6291460
  11.4 7.1 %collective-permute-start.2 = (bf16[128,1024]{1,0:T(8,128)(2,1)S(1)}, bf16[128,1024]{1,0:T(8,128)(2,1)S(1)}, u32[]{:S(2)}, u32[]{:S(2)}) collective-permute-start(bf16[128,1024]{1,0:T(8,128)(2,1)S(1)} %broadcast_select_fusion), channel_id=1, source_target_pairs={{0,1},{1,0},{2,3},{3,2},{8,10},{9,11},{10,8},{11,9},{16,17},{17,16... | collective-permute-start | bytes 786440 | tf_op jit(solution)/shard_map/ppermute | solution.py:144
  14.0 4.5 %copy-start.2 = (s32[4]{0:T(128)S(1)}, s32[4]{0:T(128)}, u32[]{:S(2)}) copy-start(s32[4]{0:T(128)} %param.7) | copy-start | bytes 52

commit v6 on v5

--- a/solution.py
+++ b/solution.py
@@ -79,15 +79,13 @@
 def place_kernel(ny, half, in_ref, out_ref, placed, sems):
     channels = in_ref.shape[0]
     deep = in_ref.shape[2]
-    first = lax.broadcasted_iota(jnp.int32, (deep, 2 * half), 1) < half
     copies = []
     for c in range(channels):
         for y in range(ny):
-            a, b = in_ref[c, y].astype(F32), in_ref[c, ny + y].astype(F32)
-            top = jnp.where(first, a, pltpu.roll(b, half, 1))
-            bottom = jnp.where(first, pltpu.roll(a, half, 1), b)
-            placed[c, :deep, y * 2 * half : (y + 1) * 2 * half] = top.astype(BF16)
-            placed[c, deep:, y * 2 * half : (y + 1) * 2 * half] = bottom.astype(BF16)
+            a, b = in_ref[c, y], in_ref[c, ny + y]
+            at = slice(y * 2 * half, (y + 1) * 2 * half)
+            placed[c, :deep, at] = jnp.concatenate([a[:, :half], b[:, :half]], axis=1)
+            placed[c, deep:, at] = jnp.concatenate([a[:, half:], b[:, half:]], axis=1)
         copies.append(pltpu.make_async_copy(placed.at[c], out_ref.at[c], sems.at[c]))
         copies[-1].start()
     for copy in copies:

time: 31.6 us -> 31.6 us (level)
  no operation moved by 1% of the time
where the time goes in v6:
time: 31.6 us; the launch traced here: 31.4 us
  blocking collectives  11.1 us (35%)
  starting transfers between devices  10 us (32%)
  waiting for transfers between devices  4.77 us (15%)
  Pallas kernels  3.73 us (12%)
  local copies, waits for them, and re-layouts  1.01 us (3%)
  between operations  0.71 us (2%)
    all_to_all x1, blocking collectives, per_device(): lax.all_to_all(sent, ('chan', 'zp', 'y'), split_axis=0, concat_axis=0, ti...  11.1 us
    pallas_call x4, Pallas kernels, call(): pl.pallas_call(kernel, out_shape=out_shape, in_specs=[pl.BlockSpec(memory...  3.73 us
    ppermute x1, starting transfers between devices, lab_tiles(): near = lax.ppermute(t, 'zp', xor_pairs(2, 1))  3.02 us
    ppermute x1, starting transfers between devices, lab_tiles(): shares.append(lax.ppermute(same, 'zg', xor_pairs(nzg, k)))  2.65 us
    ppermute x1, starting transfers between devices, lab_tiles(): lax.ppermute(jnp.where(odd, other_line, near), ('chan', 'zp', 'y'), turn_...  2.6 us
    ppermute x1, waiting for transfers between devices, lab_tiles(): near = lax.ppermute(t, 'zp', xor_pairs(2, 1))  2.28 us
    ppermute x1, waiting for transfers between devices, lab_tiles(): shares.append(lax.ppermute(same, 'zg', xor_pairs(nzg, k)))  1.95 us
    ppermute x1, starting transfers between devices, lab_tiles(): side = [lax.ppermute(t, 'y', xor_pairs(ny, k)) for k in range(1, ny)]  1.52 us
  transfers between devices with their start and end apart: 5, of which 3 were waited for; matrix products, arithmetic and copies ran while one was open for 3% of the time, Pallas kernels for 6%

profile of v6, /device:TPU:0, one launch (start us, length us, event | category | flops | bytes accessed | tf_op | source)
XLA Modules:
  0.0 31.4 jit_solution(15249170477261079682)
XLA Ops:
  0.0 3.0 %collective-permute-start = (bf16[128,1024]{1,0:T(8,128)(2,1)}, bf16[128,1024]{1,0:T(8,128)(2,1)S(1)}, u32[]{:S(2)}, u32[]{:S(2)}) collective-permute-start(bf16[128,1024]{1,0:T(8,128)(2,1)} %bitcast.10), channel_id=1, source_target_pairs={{0,2},{2,0},{1,3},{3,1},{4,6},{6,4},{5,7},{7,5},{8,10},{10,8},{9,1... | collective-permute-start | bytes 786440 | tf_op jit(solution)/shard_map/ppermute | solution.py:129
  3.0 1.5 %collective-permute-start.1 = (bf16[128,1024]{1,0:T(8,128)(2,1)}, bf16[128,1024]{1,0:T(8,128)(2,1)S(1)}, u32[]{:S(2)}, u32[]{:S(2)}) collective-permute-start(bf16[128,1024]{1,0:T(8,128)(2,1)} %bitcast.11), channel_id=1, source_target_pairs={{0,1},{1,0},{2,3},{3,2},{4,5},{5,4},{6,7},{7,6},{8,9},{9,8},{10,11... | collective-permute-start | bytes 786440 | tf_op jit(solution)/shard_map/ppermute | solution.py:130
  4.5 1.0 %dynamic-slice_bitcast_fusion = (bf16[64,1024]{1,0:T(8,128)(2,1)S(1)}, bf16[64,1024]{1,0:T(8,128)(2,1)S(1)}) fusion(bf16[1,128,1024]{2,1,0:T(8,128)(2,1)} %param.4, s32[]{:T(128)S(6)} %select_n.25, s32[]{:T(128)S(6)} %select_n.24), kind=kLoop, calls=%fused_computation.1 | loop fusion | bytes 524296 | tf_op jit(solution)/shard_map/dynamic_slice | solution.py:132
  5.5 2.7 %collective-permute-start.3 = (bf16[64,1024]{1,0:T(8,128)(2,1)S(1)}, bf16[64,1024]{1,0:T(8,128)(2,1)S(1)}, u32[]{:S(2)}, u32[]{:S(2)}) collective-permute-start(bf16[64,1024]{1,0:T(8,128)(2,1)S(1)} %get-tuple-element.18.refs_1_), channel_id=1, source_target_pairs={{0,4},{4,0},{1,5},{5,1},{2,6},{6,2},{3,7},{7,3},{8,12},{12,8},{9,1... | collective-permute-start | bytes 393224 | tf_op jit(solution)/shard_map/ppermute | solution.py:135
  8.2 0.2 collective-permute-start.4
  9.1 2.3 %collective-permute-done.refs_2_.near_ref = bf16[128,1024]{1,0:T(8,128)(2,1)S(1)} collective-permute-done((bf16[128,1024]{1,0:T(8,128)(2,1)}, bf16[128,1024]{1,0:T(8,128)(2,1)S(1)}, u32[]{:S(2)}, u32[]{:S(2)}) %collective-permute-start) | collective-permute-done | bytes 262176 | tf_op jit(solution)/shard_map/ppermute | solution.py:129
  11.4 0.0 copy-start
  11.4 0.0 copy-start.1
  11.4 0.0 collective-permute-done.1.refs_1_
  11.4 2.6 %collective-permute-start.2 = (bf16[128,1024]{1,0:T(8,128)(2,1)S(1)}, bf16[128,1024]{1,0:T(8,128)(2,1)S(1)}, u32[]{:S(2)}, u32[]{:S(2)}) collective-permute-start(bf16[128,1024]{1,0:T(8,128)(2,1)S(1)} %broadcast_select_fusion), channel_id=1, source_target_pairs={{0,1},{1,0},{2,3},{3,2},{8,10},{9,11},{10,8},{11,9},{16,17},{17,16... | collective-permute-start | bytes 786440 | tf_op jit(solution)/shard_map/ppermute | solution.py:142
  14.0 0.0 copy-done
  14.0 0.0 copy-done.1
  14.0 0.0 copy-start.2
  14.0 2.0 %shard_map.47 = (bf16[1024,1024]{1,0:T(8,128)(2,1)S(1)}, bf16[384,1024]{1,0:T(8,128)(2,1)S(1)}) custom-call(s32[1]{0:T(128)S(6)} %copy.5.live_ref, bf16[1024,1024]{1,0:T(8,128)(2,1)S(1)} %bitcast.15, bf16[128,1024]{1,0:T(8,128)(2,1)S(1)} %bitcast.12, bf16[128,1024]{1,0:T(8,128)(2,1)S(1)} %collective-permute-done.1.refs_1_, ...), custom_call_target="tpu_custom_call" | custom-call | flops 99999997952 | bytes 99999997952 | tf_op jit(solution)/shard_map/pallas_call | solution.py:112
  16.1 1.9 %collective-permute-done.3.refs_2_ = bf16[64,1024]{1,0:T(8,128)(2,1)S(1)} collective-permute-done((bf16[64,1024]{1,0:T(8,128)(2,1)S(1)}, bf16[64,1024]{1,0:T(8,128)(2,1)S(1)}, u32[]{:S(2)}, u32[]{:S(2)}) %collective-permute-start.3) | collective-permute-done | bytes 131104 | tf_op jit(solution)/shard_map/ppermute | solution.py:135
  18.0 0.5 %collective-permute-done.4.refs_3_ = bf16[64,1024]{1,0:T(8,128)(2,1)S(1)} collective-permute-done((bf16[64,1024]{1,0:T(8,128)(2,1)S(1)}, bf16[64,1024]{1,0:T(8,128)(2,1)S(1)}, u32[]{:S(2)}, u32[]{:S(2)}) %collective-permute-start.4) | collective-permute-done | bytes 131104 | tf_op jit(solution)/shard_map/ppermute | solution.py:136
  18.5 0.0 collective-permute-done.2.refs_0_
  18.5 0.0 copy-done.2
  18.5 0.9 %shard_map.48 = bf16[4,4,64,128]{3,2,1,0:T(8,128)(2,1)S(1)} custom-call(s32[1,4]{1,0:T(1,128)S(1)} %shard_map.46.order_ref, s32[1,4]{1,0:T(1,128)S(1)} %bitcast.16, bf16[384,1024]{1,0:T(8,128)(2,1)S(1)} %get-tuple-element.15.w_ref, bf16[1024,1024]{1,0:T(8,128)(2,1)S(1)} %get-tuple-element.16.vm_ref, ...), custom_call_target="tpu_custom_call" | custom-call | flops 99999997952 | bytes 99999997952 | tf_op jit(solution)/shard_map/pallas_call | solution.py:112
  19.4 11.1 %all_to_all.5 = bf16[16,64,128]{2,1,0:T(8,128)(2,1)S(1)} all-to-all(bf16[16,64,128]{2,1,0:T(8,128)(2,1)S(1)} %bitcast.13), channel_id=1, replica_groups=mesh['chan'=4,'zg'=2,'zp'=2,'y'=2] {'chan','zp','y'}, dimensions={0} | all-to-all | bytes 524288 | tf_op jit(solution)/shard_map/all_to_all | solution.py:169
  30.6 0.8 %shard_map.49 = bf16[4,128,256]{2,1,0:T(8,128)(2,1)} custom-call(bf16[4,4,64,128]{3,2,1,0:T(8,128)(2,1)S(1)} %bitcast.14), custom_call_target="tpu_custom_call" | custom-call | flops 99999997952 | bytes 99999997952 | tf_op jit(solution)/shard_map/pallas_call | solution.py:112
  (3 shorter events, 0.0 us)
Async XLA Ops:
  0.0 11.4 %collective-permute-start = (bf16[128,1024]{1,0:T(8,128)(2,1)}, bf16[128,1024]{1,0:T(8,128)(2,1)S(1)}, u32[]{:S(2)}, u32[]{:S(2)}) collective-permute-start(bf16[128,1024]{1,0:T(8,128)(2,1)} %bitcast.10), channel_id=1, source_target_pairs={{0,2},{2,0},{1,3},{3,1},{4,6},{6,4},{5,7},{7,5},{8,10},{10,8},{9,1... | collective-permute-start | bytes 786440 | tf_op jit(solution)/shard_map/ppermute | solution.py:129
  3.0 8.4 %collective-permute-start.1 = (bf16[128,1024]{1,0:T(8,128)(2,1)}, bf16[128,1024]{1,0:T(8,128)(2,1)S(1)}, u32[]{:S(2)}, u32[]{:S(2)}) collective-permute-start(bf16[128,1024]{1,0:T(8,128)(2,1)} %bitcast.11), channel_id=1, source_target_pairs={{0,1},{1,0},{2,3},{3,2},{4,5},{5,4},{6,7},{7,6},{8,9},{9,8},{10,11... | collective-permute-start | bytes 786440 | tf_op jit(solution)/shard_map/ppermute | solution.py:130
  5.5 12.5 %collective-permute-start.3 = (bf16[64,1024]{1,0:T(8,128)(2,1)S(1)}, bf16[64,1024]{1,0:T(8,128)(2,1)S(1)}, u32[]{:S(2)}, u32[]{:S(2)}) collective-permute-start(bf16[64,1024]{1,0:T(8,128)(2,1)S(1)} %get-tuple-element.18.refs_1_), channel_id=1, source_target_pairs={{0,4},{4,0},{1,5},{5,1},{2,6},{6,2},{3,7},{7,3},{8,12},{12,8},{9,1... | collective-permute-start | bytes 393224 | tf_op jit(solution)/shard_map/ppermute | solution.py:135
  8.2 10.3 %collective-permute-start.4 = (bf16[64,1024]{1,0:T(8,128)(2,1)S(1)}, bf16[64,1024]{1,0:T(8,128)(2,1)S(1)}, u32[]{:S(2)}, u32[]{:S(2)}) collective-permute-start(bf16[64,1024]{1,0:T(8,128)(2,1)S(1)} %get-tuple-element.17), channel_id=1, source_target_pairs={{0,6},{2,4},{4,2},{6,0},{1,7},{3,5},{5,3},{7,1},{8,14},{10,12},{12... | collective-permute-start | bytes 393224 | tf_op jit(solution)/shard_map/ppermute | solution.py:136
  11.4 2.7 %copy-start = (bf16[1,128,1024]{2,1,0:T(8,128)(2,1)S(1)}, bf16[1,128,1024]{2,1,0:T(8,128)(2,1)}, u32[]{:S(2)}) copy-start(bf16[1,128,1024]{2,1,0:T(8,128)(2,1)} %param.4) | copy-start | bytes 786436
  11.4 2.7 %copy-start.1 = (bf16[1,1024,1024]{2,1,0:T(8,128)(2,1)S(1)}, bf16[1,1024,1024]{2,1,0:T(8,128)(2,1)}, u32[]{:S(2)}) copy-start(bf16[1,1024,1024]{2,1,0:T(8,128)(2,1)} %param.5) | copy-start | bytes 6291460
  11.4 7.1 %collective-permute-start.2 = (bf16[128,1024]{1,0:T(8,128)(2,1)S(1)}, bf16[128,1024]{1,0:T(8,128)(2,1)S(1)}, u32[]{:S(2)}, u32[]{:S(2)}) collective-permute-start(bf16[128,1024]{1,0:T(8,128)(2,1)S(1)} %broadcast_select_fusion), channel_id=1, source_target_pairs={{0,1},{1,0},{2,3},{3,2},{8,10},{9,11},{10,8},{11,9},{16,17},{17,16... | collective-permute-start | bytes 786440 | tf_op jit(solution)/shard_map/ppermute | solution.py:142
  14.0 4.5 %copy-start.2 = (s32[4]{0:T(128)S(1)}, s32[4]{0:T(128)}, u32[]{:S(2)}) copy-start(s32[4]{0:T(128)} %param.7) | copy-start | bytes 52

commit v7 on v6

--- a/solution.py
+++ b/solution.py
@@ -26,7 +26,7 @@
     t_refs, (vm_ref, w_ref) = refs[:-2], refs[-2:]
     width = v_ref.shape[0]
     tile = min(256, width)
-    live = live_ref[0]
+    live = live_ref[...]
     for i in range(0, width, tile):
         row_live = lax.broadcasted_iota(jnp.int32, (tile, tile), 0) + i < live
         for j in range(0, width, tile):
@@ -147,8 +147,7 @@
     vm, w = call(
         first_kernel,
         [jax.ShapeDtypeStruct((width, width), BF16), jax.ShapeDtypeStruct((len(lefts) * rows, width), BF16)],
-        [channel_dims, v] + lefts,
-        scalars=1,
+        [channel_dims[None, :], v] + lefts,
     )
     return call(
         functools.partial(tiles_kernel, half),

time: 31.6 us -> 31.6 us (level)
  no operation moved by 1% of the time
where the time goes in v7:
time: 31.6 us; the launch traced here: 31.4 us
  blocking collectives  11.1 us (35%)
  starting transfers between devices  10 us (32%)
  waiting for transfers between devices  4.77 us (15%)
  Pallas kernels  3.73 us (12%)
  local copies, waits for them, and re-layouts  1.01 us (3%)
  between operations  0.71 us (2%)
    all_to_all x1, blocking collectives, per_device(): lax.all_to_all(sent, ('chan', 'zp', 'y'), split_axis=0, concat_axis=0, ti...  11.1 us
    pallas_call x4, Pallas kernels, call(): pl.pallas_call(kernel, out_shape=out_shape, in_specs=[pl.BlockSpec(memory...  3.73 us
    ppermute x1, starting transfers between devices, lab_tiles(): near = lax.ppermute(t, 'zp', xor_pairs(2, 1))  3.02 us
    ppermute x1, starting transfers between devices, lab_tiles(): shares.append(lax.ppermute(same, 'zg', xor_pairs(nzg, k)))  2.65 us
    ppermute x1, starting transfers between devices, lab_tiles(): lax.ppermute(jnp.where(odd, other_line, near), ('chan', 'zp', 'y'), turn_...  2.6 us
    ppermute x1, waiting for transfers between devices, lab_tiles(): near = lax.ppermute(t, 'zp', xor_pairs(2, 1))  2.28 us
    ppermute x1, waiting for transfers between devices, lab_tiles(): shares.append(lax.ppermute(same, 'zg', xor_pairs(nzg, k)))  1.95 us
    ppermute x1, starting transfers between devices, lab_tiles(): side = [lax.ppermute(t, 'y', xor_pairs(ny, k)) for k in range(1, ny)]  1.52 us
  transfers between devices with their start and end apart: 5, of which 3 were waited for; matrix products, arithmetic and copies ran while one was open for 3% of the time, Pallas kernels for 6%

profile of v7, /device:TPU:0, one launch (start us, length us, event | category | flops | bytes accessed | tf_op | source)
XLA Modules:
  0.0 31.4 jit_solution(15669687962515818336)
XLA Ops:
  0.0 3.0 %collective-permute-start = (bf16[128,1024]{1,0:T(8,128)(2,1)}, bf16[128,1024]{1,0:T(8,128)(2,1)S(1)}, u32[]{:S(2)}, u32[]{:S(2)}) collective-permute-start(bf16[128,1024]{1,0:T(8,128)(2,1)} %bitcast.12), channel_id=1, source_target_pairs={{0,2},{2,0},{1,3},{3,1},{4,6},{6,4},{5,7},{7,5},{8,10},{10,8},{9,1... | collective-permute-start | bytes 786440 | tf_op jit(solution)/shard_map/ppermute | solution.py:129
  3.0 1.5 %collective-permute-start.1 = (bf16[128,1024]{1,0:T(8,128)(2,1)}, bf16[128,1024]{1,0:T(8,128)(2,1)S(1)}, u32[]{:S(2)}, u32[]{:S(2)}) collective-permute-start(bf16[128,1024]{1,0:T(8,128)(2,1)} %bitcast.13), channel_id=1, source_target_pairs={{0,1},{1,0},{2,3},{3,2},{4,5},{5,4},{6,7},{7,6},{8,9},{9,8},{10,11... | collective-permute-start | bytes 786440 | tf_op jit(solution)/shard_map/ppermute | solution.py:130
  4.5 1.0 %dynamic-slice_bitcast_fusion = (bf16[64,1024]{1,0:T(8,128)(2,1)S(1)}, bf16[64,1024]{1,0:T(8,128)(2,1)S(1)}) fusion(bf16[1,128,1024]{2,1,0:T(8,128)(2,1)} %param.4, s32[]{:T(128)S(6)} %select_n.25, s32[]{:T(128)S(6)} %select_n.24), kind=kLoop, calls=%fused_computation.1 | loop fusion | bytes 524296 | tf_op jit(solution)/shard_map/dynamic_slice | solution.py:132
  5.5 2.7 %collective-permute-start.3 = (bf16[64,1024]{1,0:T(8,128)(2,1)S(1)}, bf16[64,1024]{1,0:T(8,128)(2,1)S(1)}, u32[]{:S(2)}, u32[]{:S(2)}) collective-permute-start(bf16[64,1024]{1,0:T(8,128)(2,1)S(1)} %get-tuple-element.18.refs_1_), channel_id=1, source_target_pairs={{0,4},{4,0},{1,5},{5,1},{2,6},{6,2},{3,7},{7,3},{8,12},{12,8},{9,1... | collective-permute-start | bytes 393224 | tf_op jit(solution)/shard_map/ppermute | solution.py:135
  8.2 0.2 collective-permute-start.4
  9.1 2.3 %collective-permute-done.refs_2_.near_ref = bf16[128,1024]{1,0:T(8,128)(2,1)S(1)} collective-permute-done((bf16[128,1024]{1,0:T(8,128)(2,1)}, bf16[128,1024]{1,0:T(8,128)(2,1)S(1)}, u32[]{:S(2)}, u32[]{:S(2)}) %collective-permute-start) | collective-permute-done | bytes 262176 | tf_op jit(solution)/shard_map/ppermute | solution.py:129
  11.4 0.0 copy-start
  11.4 0.0 copy-start.1
  11.4 0.0 collective-permute-done.1.refs_1_
  11.4 2.6 %collective-permute-start.2 = (bf16[128,1024]{1,0:T(8,128)(2,1)S(1)}, bf16[128,1024]{1,0:T(8,128)(2,1)S(1)}, u32[]{:S(2)}, u32[]{:S(2)}) collective-permute-start(bf16[128,1024]{1,0:T(8,128)(2,1)S(1)} %broadcast_select_fusion), channel_id=1, source_target_pairs={{0,1},{1,0},{2,3},{3,2},{8,10},{9,11},{10,8},{11,9},{16,17},{17,16... | collective-permute-start | bytes 786440 | tf_op jit(solution)/shard_map/ppermute | solution.py:142
  14.0 0.0 copy-done
  14.0 0.0 copy-done.1
  14.0 0.0 copy-start.2
  14.0 2.0 %shard_map.47 = (bf16[1024,1024]{1,0:T(8,128)(2,1)S(1)}, bf16[384,1024]{1,0:T(8,128)(2,1)S(1)}) custom-call(s32[1,1]{1,0:T(1,128)} %bitcast.11.live_ref, bf16[1024,1024]{1,0:T(8,128)(2,1)S(1)} %bitcast.17, bf16[128,1024]{1,0:T(8,128)(2,1)S(1)} %bitcast.14, bf16[128,1024]{1,0:T(8,128)(2,1)S(1)} %collective-permute-done.1.refs_1_, ...), custom_call_target="tpu_custom_call" | custom-call | flops 99999997952 | bytes 99999997952 | tf_op jit(solution)/shard_map/pallas_call | solution.py:112
  16.1 2.0 %collective-permute-done.3.refs_2_ = bf16[64,1024]{1,0:T(8,128)(2,1)S(1)} collective-permute-done((bf16[64,1024]{1,0:T(8,128)(2,1)S(1)}, bf16[64,1024]{1,0:T(8,128)(2,1)S(1)}, u32[]{:S(2)}, u32[]{:S(2)}) %collective-permute-start.3) | collective-permute-done | bytes 131104 | tf_op jit(solution)/shard_map/ppermute | solution.py:135
  18.0 0.5 %collective-permute-done.4.refs_3_ = bf16[64,1024]{1,0:T(8,128)(2,1)S(1)} collective-permute-done((bf16[64,1024]{1,0:T(8,128)(2,1)S(1)}, bf16[64,1024]{1,0:T(8,128)(2,1)S(1)}, u32[]{:S(2)}, u32[]{:S(2)}) %collective-permute-start.4) | collective-permute-done | bytes 131104 | tf_op jit(solution)/shard_map/ppermute | solution.py:136
  18.5 0.0 collective-permute-done.2.refs_0_
  18.5 0.0 copy-done.2
  18.5 0.9 %shard_map.48 = bf16[4,4,64,128]{3,2,1,0:T(8,128)(2,1)S(1)} custom-call(s32[1,4]{1,0:T(1,128)S(1)} %shard_map.46.order_ref, s32[1,4]{1,0:T(1,128)S(1)} %bitcast.18, bf16[384,1024]{1,0:T(8,128)(2,1)S(1)} %get-tuple-element.15.w_ref, bf16[1024,1024]{1,0:T(8,128)(2,1)S(1)} %get-tuple-element.16.vm_ref, ...), custom_call_target="tpu_custom_call" | custom-call | flops 99999997952 | bytes 99999997952 | tf_op jit(solution)/shard_map/pallas_call | solution.py:112
  19.4 11.1 %all_to_all.5 = bf16[16,64,128]{2,1,0:T(8,128)(2,1)S(1)} all-to-all(bf16[16,64,128]{2,1,0:T(8,128)(2,1)S(1)} %bitcast.15), channel_id=1, replica_groups=mesh['chan'=4,'zg'=2,'zp'=2,'y'=2] {'chan','zp','y'}, dimensions={0} | all-to-all | bytes 524288 | tf_op jit(solution)/shard_map/all_to_all | solution.py:168
  30.6 0.8 %shard_map.49 = bf16[4,128,256]{2,1,0:T(8,128)(2,1)} custom-call(bf16[4,4,64,128]{3,2,1,0:T(8,128)(2,1)S(1)} %bitcast.16), custom_call_target="tpu_custom_call" | custom-call | flops 99999997952 | bytes 99999997952 | tf_op jit(solution)/shard_map/pallas_call | solution.py:112
  (3 shorter events, 0.0 us)
Async XLA Ops:
  0.0 11.4 %collective-permute-start = (bf16[128,1024]{1,0:T(8,128)(2,1)}, bf16[128,1024]{1,0:T(8,128)(2,1)S(1)}, u32[]{:S(2)}, u32[]{:S(2)}) collective-permute-start(bf16[128,1024]{1,0:T(8,128)(2,1)} %bitcast.12), channel_id=1, source_target_pairs={{0,2},{2,0},{1,3},{3,1},{4,6},{6,4},{5,7},{7,5},{8,10},{10,8},{9,1... | collective-permute-start | bytes 786440 | tf_op jit(solution)/shard_map/ppermute | solution.py:129
  3.0 8.4 %collective-permute-start.1 = (bf16[128,1024]{1,0:T(8,128)(2,1)}, bf16[128,1024]{1,0:T(8,128)(2,1)S(1)}, u32[]{:S(2)}, u32[]{:S(2)}) collective-permute-start(bf16[128,1024]{1,0:T(8,128)(2,1)} %bitcast.13), channel_id=1, source_target_pairs={{0,1},{1,0},{2,3},{3,2},{4,5},{5,4},{6,7},{7,6},{8,9},{9,8},{10,11... | collective-permute-start | bytes 786440 | tf_op jit(solution)/shard_map/ppermute | solution.py:130
  5.5 12.5 %collective-permute-start.3 = (bf16[64,1024]{1,0:T(8,128)(2,1)S(1)}, bf16[64,1024]{1,0:T(8,128)(2,1)S(1)}, u32[]{:S(2)}, u32[]{:S(2)}) collective-permute-start(bf16[64,1024]{1,0:T(8,128)(2,1)S(1)} %get-tuple-element.18.refs_1_), channel_id=1, source_target_pairs={{0,4},{4,0},{1,5},{5,1},{2,6},{6,2},{3,7},{7,3},{8,12},{12,8},{9,1... | collective-permute-start | bytes 393224 | tf_op jit(solution)/shard_map/ppermute | solution.py:135
  8.2 10.3 %collective-permute-start.4 = (bf16[64,1024]{1,0:T(8,128)(2,1)S(1)}, bf16[64,1024]{1,0:T(8,128)(2,1)S(1)}, u32[]{:S(2)}, u32[]{:S(2)}) collective-permute-start(bf16[64,1024]{1,0:T(8,128)(2,1)S(1)} %get-tuple-element.17), channel_id=1, source_target_pairs={{0,6},{2,4},{4,2},{6,0},{1,7},{3,5},{5,3},{7,1},{8,14},{10,12},{12... | collective-permute-start | bytes 393224 | tf_op jit(solution)/shard_map/ppermute | solution.py:136
  11.4 2.7 %copy-start = (bf16[1,128,1024]{2,1,0:T(8,128)(2,1)S(1)}, bf16[1,128,1024]{2,1,0:T(8,128)(2,1)}, u32[]{:S(2)}) copy-start(bf16[1,128,1024]{2,1,0:T(8,128)(2,1)} %param.4) | copy-start | bytes 786436
  11.4 2.7 %copy-start.1 = (bf16[1,1024,1024]{2,1,0:T(8,128)(2,1)S(1)}, bf16[1,1024,1024]{2,1,0:T(8,128)(2,1)}, u32[]{:S(2)}) copy-start(bf16[1,1024,1024]{2,1,0:T(8,128)(2,1)} %param.5) | copy-start | bytes 6291460
  11.4 7.1 %collective-permute-start.2 = (bf16[128,1024]{1,0:T(8,128)(2,1)S(1)}, bf16[128,1024]{1,0:T(8,128)(2,1)S(1)}, u32[]{:S(2)}, u32[]{:S(2)}) collective-permute-start(bf16[128,1024]{1,0:T(8,128)(2,1)S(1)} %broadcast_select_fusion), channel_id=1, source_target_pairs={{0,1},{1,0},{2,3},{3,2},{8,10},{9,11},{10,8},{11,9},{16,17},{17,16... | collective-permute-start | bytes 786440 | tf_op jit(solution)/shard_map/ppermute | solution.py:142
  14.0 4.5 %copy-start.2 = (s32[4]{0:T(128)S(1)}, s32[4]{0:T(128)}, u32[]{:S(2)}) copy-start(s32[4]{0:T(128)} %param.7) | copy-start | bytes 52
